TPU v7x, 128 devices: a whole 4x4x4 slice. The times are simulated.
128 devices in a mesh: row: 16 (over z, x_lo, core), col: 8 (over x_hi, y).
Axes of the slice: x: 4 (x_hi: 2, x_lo: 2; x = x_hi * 2 + x_lo), y: 4, z: 4, core: 2. Of those that a mesh axis runs over, the one named last changes fastest.
Arguments:
- tile_values: bfloat16 [32768, 128, 128], P(('row', 'col')), may hold values from -0.09375 to 0.09375
- slot_codes: int32 [32768], P(('row', 'col')), may hold values from -1 to 511, as said below
- right_start: float32 [32768, 256], P(('row', 'col')), may hold values from -6 to 6
- left_start: float32 [32768, 256], P(('row', 'col')), may hold values from -6 to 6
- node_diagonal: float32 [32768], P(('row', 'col')), may hold values from 1 to 3
- row_scale: float32 [32768], P(('row', 'col')), may hold values from 0.2 to 15
Outputs:
- right_block: float32 [32768, 256], P(('row', 'col'))
- left_block: float32 [32768, 256], P(('row', 'col'))
- projections: float32 [2, 256, 256], replicated
Inputs may be any that keep to these rules, and one draw needn't show every extreme that they name: `slot_codes`: slot (s, p, c) carries a tile that device s extracted for owner p; its code is -1 (empty) or a position a 32 + b in p's block grid of 16 x 2 * 16 places. The codes of one owner's live slots over all sources are distinct, so an owner receives at most 128 live tiles, and some owner receives exactly 128. A source fills at most 2 slots for one owner, and some source fills all 2.
All inputs are finite; a program needn't handle non-finite values.
Results may differ from a plain program's by a relative error of at most 0.002.
Values may be sent and summed in bfloat16 or wider, within the bound.
A program may use at most 128 MiB of HBM per device.

v0:
```python
import jax
import jax.numpy as jnp
from jax import lax
from jax.sharding import PartitionSpec as P

ITERS = 2


epsilon = 1e-06


def slot_product(slot_tiles, pick_keys, sum_keys, blocks, key_count, transposed):
    tile_rows = slot_tiles.shape[1]
    port_count = blocks.shape[2]
    slot_total = slot_tiles.shape[0]
    groups = 4
    grouped_tiles = slot_tiles.reshape(groups, slot_total // groups, tile_rows, tile_rows)
    grouped_pick = pick_keys.reshape(groups, slot_total // groups)
    grouped_sum = sum_keys.reshape(groups, slot_total // groups)
    form = "syx,syp->sxp" if transposed else "sxy,syp->sxp"

    def accumulate(summed, group):
        group_tiles, group_pick, group_sum = group
        picked = blocks[group_pick]
        contrib = jnp.einsum(form, group_tiles, picked, preferred_element_type=jnp.float32)
        onehot = (group_sum[:, None] == jnp.arange(key_count)[None, :]).astype(jnp.float32)
        added = jnp.einsum("sn,sxp->nxp", onehot, contrib, precision=lax.Precision.HIGHEST)
        return (summed + added, None)

    start = jnp.zeros((key_count, tile_rows, port_count), jnp.float32)
    summed, _ = lax.scan(accumulate, start, (grouped_tiles, grouped_pick, grouped_sum))
    return summed.reshape(key_count * tile_rows, port_count)


def local(tile_values, slot_codes, right_start, left_start, node_diagonal, row_scale):
    row_size = lax.axis_size("row")
    col_size = lax.axis_size("col")
    owners = row_size * col_size
    tile_rows = tile_values.shape[1]
    port_count = right_start.shape[1]
    order_rows = right_start.shape[0] * owners
    grid_rows = 2 * col_size
    grid_cols = 2 * row_size
    got_tiles, got_codes = (
        lax.all_to_all(tile_values, ("row", "col"), split_axis=0, concat_axis=0, tiled=True),
        lax.all_to_all(slot_codes, ("row", "col"), split_axis=0, concat_axis=0, tiled=True),
    )
    live = got_codes >= 0
    block_row = got_codes // grid_cols
    block_col = got_codes % grid_cols
    row_sum_key = jnp.where(live, block_row, grid_rows)
    col_pick_key = jnp.where(live, block_col, 0)
    row_pick_key = jnp.where(live, block_row, 0)
    col_sum_key = jnp.where(live, block_col, grid_cols)
    scale_col = row_scale[:, None]
    diag_col = node_diagonal[:, None]
    right_vec = right_start
    left_vec = right_start + left_start
    stored = []
    for turn in range(ITERS):
        right_bf = right_vec.astype(jnp.bfloat16)
        scaled_left = scale_col * left_vec
        left_bf = scaled_left.astype(jnp.bfloat16)
        right_cols = lax.all_gather(right_bf, "row", axis=0, tiled=True)
        left_rows = lax.all_gather(left_bf, "col", axis=0, tiled=True)
        right_blocks = right_cols.reshape(grid_cols, tile_rows, port_count)
        right_part = slot_product(
            got_tiles, col_pick_key, row_sum_key, right_blocks, grid_rows, False
        )
        blocks = left_rows.reshape(grid_rows, tile_rows, port_count)
        left_part = slot_product(got_tiles, row_pick_key, col_sum_key, blocks, grid_cols, True)
        right_prod = lax.psum_scatter(right_part, "col", scatter_dimension=0, tiled=True)
        left_prod = lax.psum_scatter(left_part, "row", scatter_dimension=0, tiled=True)
        right_new = scale_col * (right_prod + diag_col * right_vec)
        left_new = left_prod + diag_col * scaled_left
        local_proj = jnp.dot(left_vec.T, right_new, precision=lax.Precision.HIGHEST)
        project = lax.psum(local_proj, ("row", "col")) / order_rows
        right_rest = right_new - jnp.dot(right_vec, project, precision=lax.Precision.HIGHEST)
        left_rest = left_new - jnp.dot(left_vec, project.T, precision=lax.Precision.HIGHEST)
        right_sq, left_sq = lax.psum(
            (jnp.sum(right_rest * right_rest, axis=0), jnp.sum(left_rest * left_rest, axis=0)),
            ("row", "col"),
        )
        right_vec = right_rest / jnp.sqrt(right_sq / order_rows + epsilon)[None, :]
        left_vec = left_rest / jnp.sqrt(left_sq / order_rows + epsilon)[None, :]
        stored.append(project)
    return (right_vec, left_vec, jnp.stack(stored))


def solution(mesh):
    return jax.shard_map(
        local,
        mesh=mesh,
        in_specs=(
            P(("row", "col"), None, None),
            P(("row", "col")),
            P(("row", "col"), None),
            P(("row", "col"), None),
            P(("row", "col")),
            P(("row", "col")),
        ),
        out_specs=(P(("row", "col"), None), P(("row", "col"), None), P()),
        check_vma=False,
    )
```

profile of v0, /device:TPU:1, one launch (start us, length us, event | category | flops | bytes accessed | tf_op | source)
XLA Modules:
  0.0 1186.2 jit_solution(6084935444073180689)
XLA Ops:
  8.0 21.1 %all_to_all.17 = s32[128,2,1]{1,2,0:T(1,128)S(1)} all-to-all(s32[128,2,1]{1,2,0:T(1,128)S(1)} %bitcast.149), channel_id=1, replica_groups=mesh['row'=16,'col'=8] {'row','col'}, dimensions={0} | all-to-all | bytes 2048 | tf_op jit(solution)/shard_map/all_to_all | solution.py:46
  36.8 112.9 %all-gather.5.cloned.1.call-done = bf16[4096,256]{1,0:T(8,128)(2,1)} async-done(((bf16[256,256]{1,0:T(8,128)(2,1)}), bf16[4096,256]{1,0:T(8,128)(2,1)}) %all-gather.5.cloned.1.call-update) | async-done | bytes 2097168 | tf_op jit(solution)/shard_map/all_gather | solution.py:64
  149.7 90.1 %while.44 = (s32[]{:T(128)}, f32[16,128,256]{2,0,1:T(8,128)S(1)}, s32[4,64]{1,0:T(4,128)S(1)}, bf16[4,64,128,128]{3,2,1,0:T(8,128)(2,1)}, s32[4,64]{1,0:T(4,128)...) while((s32[]{:T(128)}, f32[16,128,256]{2,0,1:T(8,128)S(1)}, ...), condition=%wide.region_1.2_spmd.clone, body=%wide.region_0.1_spmd.clone.sunk | while | flops 940574912 | bytes 35658084 | solution.py:31
  255.1 61.6 %reduce-scatter.5.cloned.1.call-done = f32[256,256]{1,0:T(8,128)} async-done(((f32[2048,256]{1,0:T(8,128)}), f32[256,256]{1,0:T(8,128)}) %reduce-scatter.5.cloned.1.call-update) | async-done | bytes 262160 | tf_op jit(solution)/shard_map/reduce_scatter | solution.py:72
  319.7 45.1 %all-gather.9.cloned.1.call-done = bf16[2048,256]{1,0:T(8,128)(2,1)} async-done(((bf16[256,256]{1,0:T(8,128)(2,1)}), bf16[2048,256]{1,0:T(8,128)(2,1)}) %all-gather.9.cloned.1.call-update) | async-done | bytes 1048592 | tf_op jit(solution)/shard_map/all_gather | solution.py:65
  364.8 101.9 %while.46 = (s32[]{:T(128)}, f32[32,128,256]{2,0,1:T(8,128)}, s32[4,64]{1,0:T(4,128)S(1)}, bf16[4,64,128,128]{2,3,1,0:T(8,128)(2,1)}, s32[4,64]{1,0:T(4,128)S(1)...) while((s32[]{:T(128)}, f32[32,128,256]{2,0,1:T(8,128)}, s32[4,64]{1,0:T(4,128)S(1)}, ...), condition=%wide.region_10.11_spmd.clone, body=%wide.region_9.10_spmd.clone.sunk | while | flops 1344277760 | bytes 39852388 | solution.py:31
  376.1 13.3 %select_add_fusion.10 = f32[32,128,256]{2,0,1:T(8,128)} fusion(f32[32,128,256]{2,0,1:T(8,128)} %get-tuple-element.481, f32[64,128,256]{2,1,0:T(8,128)} %fusion.131, pred[]{:T(512)S(6)} %compare.21, s32[64]{0:T(128)S(1)} %fusion.132), kind=kOutput, calls=%fused_computation.40.clone.1 | convolution fusion | flops 807405568 | bytes 16777472 | tf_op jit(solution)/shard_map/while/body/eval_jaxpr/sn,sxp->nxp/dot_general | solution.py:27
  400.7 14.4 %select_add_fusion.10 = f32[32,128,256]{2,0,1:T(8,128)} fusion(f32[32,128,256]{2,0,1:T(8,128)} %get-tuple-element.481, f32[64,128,256]{2,1,0:T(8,128)} %fusion.131, pred[]{:T(512)S(6)} %compare.21, s32[64]{0:T(128)S(1)} %fusion.132), kind=kOutput, calls=%fused_computation.40.clone.1 | convolution fusion | flops 807405568 | bytes 16777472 | tf_op jit(solution)/shard_map/while/body/eval_jaxpr/sn,sxp->nxp/dot_general | solution.py:27
  426.4 14.4 %select_add_fusion.10 = f32[32,128,256]{2,0,1:T(8,128)} fusion(f32[32,128,256]{2,0,1:T(8,128)} %get-tuple-element.481, f32[64,128,256]{2,1,0:T(8,128)} %fusion.131, pred[]{:T(512)S(6)} %compare.21, s32[64]{0:T(128)S(1)} %fusion.132), kind=kOutput, calls=%fused_computation.40.clone.1 | convolution fusion | flops 807405568 | bytes 16777472 | tf_op jit(solution)/shard_map/while/body/eval_jaxpr/sn,sxp->nxp/dot_general | solution.py:27
  452.1 14.4 %select_add_fusion.10 = f32[32,128,256]{2,0,1:T(8,128)} fusion(f32[32,128,256]{2,0,1:T(8,128)} %get-tuple-element.481, f32[64,128,256]{2,1,0:T(8,128)} %fusion.131, pred[]{:T(512)S(6)} %compare.21, s32[64]{0:T(128)S(1)} %fusion.132), kind=kOutput, calls=%fused_computation.40.clone.1 | convolution fusion | flops 807405568 | bytes 16777472 | tf_op jit(solution)/shard_map/while/body/eval_jaxpr/sn,sxp->nxp/dot_general | solution.py:27
  473.4 38.5 %all-reduce.5.cloned.1.call-done = f32[256,256]{1,0:T(8,128)} async-done(((f32[256,256]{1,0:T(8,128)}), f32[256,256]{1,0:T(8,128)}) %all-reduce.5.cloned.1.call-update) | async-done | bytes 262160 | tf_op jit(solution)/shard_map/psum | solution.py:77
  513.2 66.1 %reduce-scatter.9.cloned.1.call-done = f32[256,256]{1,0:T(8,128)} async-done(((f32[4096,256]{1,0:T(8,128)}), f32[256,256]{1,0:T(8,128)}) %reduce-scatter.9.cloned.1.call-update) | async-done | bytes 262160 | tf_op jit(solution)/shard_map/reduce_scatter | solution.py:73
  580.8 67.3 %all-reduce.1 = (f32[256]{0:T(256)S(1)}, f32[256]{0:T(256)S(1)}) all-reduce(f32[256]{0:T(256)S(1)} %get-tuple-element.290, f32[256]{0:T(256)S(1)} %get-tuple-element.292), channel_id=1, replica_groups=mesh['row'=16,'col'=8] {'row','col'}, use_global_device_ids=true, to_apply=%region_5.6 | all-reduce | flops 512 | bytes 4096 | tf_op jit(solution)/shard_map/psum | solution.py:80
  648.8 31.3 %all-gather.7.cloned.1.call-done = bf16[4096,256]{1,0:T(8,128)(2,1)} async-done(((bf16[256,256]{1,0:T(8,128)(2,1)}), bf16[4096,256]{1,0:T(8,128)(2,1)}) %all-gather.7.cloned.1.call-update) | async-done | bytes 2097168 | tf_op jit(solution)/shard_map/all_gather | solution.py:64
  680.1 90.2 %while.45 = (s32[]{:T(128)}, f32[16,128,256]{2,0,1:T(8,128)S(1)}, s32[4,64]{1,0:T(4,128)S(1)}, bf16[4,64,128,128]{3,2,1,0:T(8,128)(2,1)}, s32[4,64]{1,0:T(4,128)...) while((s32[]{:T(128)}, f32[16,128,256]{2,0,1:T(8,128)S(1)}, ...), condition=%wide.region_7.8_spmd.clone, body=%wide.region_6.7_spmd.clone.sunk | while | flops 940574912 | bytes 35658084 | solution.py:31
  773.9 72.2 %reduce-scatter.7.cloned.1.call-done = f32[256,256]{1,0:T(8,128)} async-done(((f32[2048,256]{1,0:T(8,128)}), f32[256,256]{1,0:T(8,128)}) %reduce-scatter.7.cloned.1.call-update) | async-done | bytes 262160 | tf_op jit(solution)/shard_map/reduce_scatter | solution.py:72
  848.5 45.6 %all-gather.11.cloned.1.call-done = bf16[2048,256]{1,0:T(8,128)(2,1)} async-done(((bf16[256,256]{1,0:T(8,128)(2,1)}), bf16[2048,256]{1,0:T(8,128)(2,1)}) %all-gather.11.cloned.1.call-update) | async-done | bytes 1048592 | tf_op jit(solution)/shard_map/all_gather | solution.py:65
  894.1 102.2 %while.47 = (s32[]{:T(128)}, f32[32,128,256]{2,0,1:T(8,128)}, s32[4,64]{1,0:T(4,128)S(1)}, bf16[4,64,128,128]{2,3,1,0:T(8,128)(2,1)}, s32[4,64]{1,0:T(4,128)S(1)...) while((s32[]{:T(128)}, f32[32,128,256]{2,0,1:T(8,128)}, s32[4,64]{1,0:T(4,128)S(1)}, ...), condition=%wide.region_18.19_spmd.clone, body=%wide.region_17.18_spmd.clone.sunk | while | flops 1344277760 | bytes 39852388 | solution.py:31
  930.2 14.4 %select_add_fusion.11 = f32[32,128,256]{2,0,1:T(8,128)} fusion(f32[32,128,256]{2,0,1:T(8,128)} %get-tuple-element.529, f32[64,128,256]{2,1,0:T(8,128)} %fusion.138, pred[]{:T(512)S(6)} %compare.22, s32[64]{0:T(128)S(1)} %fusion.139), kind=kOutput, calls=%fused_computation.57.clone.1 | convolution fusion | flops 807405568 | bytes 16777472 | tf_op jit(solution)/shard_map/while/body/eval_jaxpr/sn,sxp->nxp/dot_general | solution.py:27
  956.0 14.4 %select_add_fusion.11 = f32[32,128,256]{2,0,1:T(8,128)} fusion(f32[32,128,256]{2,0,1:T(8,128)} %get-tuple-element.529, f32[64,128,256]{2,1,0:T(8,128)} %fusion.138, pred[]{:T(512)S(6)} %compare.22, s32[64]{0:T(128)S(1)} %fusion.139), kind=kOutput, calls=%fused_computation.57.clone.1 | convolution fusion | flops 807405568 | bytes 16777472 | tf_op jit(solution)/shard_map/while/body/eval_jaxpr/sn,sxp->nxp/dot_general | solution.py:27
  981.7 14.4 %select_add_fusion.11 = f32[32,128,256]{2,0,1:T(8,128)} fusion(f32[32,128,256]{2,0,1:T(8,128)} %get-tuple-element.529, f32[64,128,256]{2,1,0:T(8,128)} %fusion.138, pred[]{:T(512)S(6)} %compare.22, s32[64]{0:T(128)S(1)} %fusion.139), kind=kOutput, calls=%fused_computation.57.clone.1 | convolution fusion | flops 807405568 | bytes 16777472 | tf_op jit(solution)/shard_map/while/body/eval_jaxpr/sn,sxp->nxp/dot_general | solution.py:27
  1003.9 37.4 %all-reduce.7.cloned.1.call-done = f32[256,256]{1,0:T(8,128)} async-done(((f32[256,256]{1,0:T(8,128)}), f32[256,256]{1,0:T(8,128)}) %all-reduce.7.cloned.1.call-update) | async-done | bytes 262160 | tf_op jit(solution)/shard_map/psum | solution.py:77
  1044.5 64.3 %reduce-scatter.11.cloned.1.call-done = f32[256,256]{1,0:T(8,128)} async-done(((f32[4096,256]{1,0:T(8,128)}), f32[256,256]{1,0:T(8,128)}) %reduce-scatter.11.cloned.1.call-update) | async-done | bytes 262160 | tf_op jit(solution)/shard_map/reduce_scatter | solution.py:73
  1110.2 67.3 %all-reduce = (f32[256]{0:T(256)S(1)}, f32[256]{0:T(256)S(1)}) all-reduce(f32[256]{0:T(256)S(1)} %get-tuple-element.294, f32[256]{0:T(256)S(1)} %get-tuple-element.296), channel_id=1, replica_groups=mesh['row'=16,'col'=8] {'row','col'}, use_global_device_ids=true, to_apply=%region_16.17 | all-reduce | flops 512 | bytes 4096 | tf_op jit(solution)/shard_map/psum | solution.py:80
  (156 shorter events, 340.1 us)
Async XLA Ops:
  29.1 5.4 copy-start.1
  29.1 5.4 copy-start.3
  29.1 5.4 copy-start.4
  29.1 120.6 %all-to-all-start.1 = ((bf16[256,128,128]{2,1,0:T(8,128)(2,1)}), bf16[256,128,128]{2,1,0:T(8,128)(2,1)}, u32[]{:S(2)}, u32[]{:S(2)}) async-start(bf16[256,128,128]{2,1,0:T(8,128)(2,1)} %param.14), calls=%async_computation.1 | async-start | bytes 16777216 | tf_op jit(solution)/shard_map/all_to_all | solution.py:45
  34.4 115.3 %all-gather.5.cloned.1.call-start = ((), (), s32[]{:S(2)}) async-start(), calls=%async_computation.6 | async-start | bytes 2228224 | tf_op jit(solution)/shard_map/all_gather | solution.py:64
  35.3 281.5 %reduce-scatter.5.cloned.1.call-start = ((), (), s32[]{:S(2)}) async-start(), calls=%async_computation.7 | async-start | bytes 2359296 | tf_op jit(solution)/shard_map/reduce_scatter | solution.py:72
  242.3 122.5 %all-gather.9.cloned.1.call-start = ((), (), s32[]{:S(2)}) async-start(), calls=%async_computation.11 | async-start | bytes 1179648 | tf_op jit(solution)/shard_map/all_gather | solution.py:65
  243.1 268.8 %all-reduce.5.cloned.1.call-start = ((), (), s32[]{:S(2)}) async-start(), calls=%async_computation.8 | async-start | bytes 524288 | tf_op jit(solution)/shard_map/psum | solution.py:77
  243.1 73.6 %copy-start.5 = (f32[256]{0:T(256)S(1)}, f32[256]{0:T(256)}, u32[]{:S(2)}) copy-start(f32[256]{0:T(256)} %param.18) | copy-start | bytes 3076
  319.1 260.2 %reduce-scatter.9.cloned.1.call-start = ((), (), s32[]{:S(2)}) async-start(), calls=%async_computation.12 | async-start | bytes 4456448 | tf_op jit(solution)/shard_map/reduce_scatter | solution.py:73
  473.3 38.6 %copy-start.2 = (f32[256,256]{1,0:T(8,128)S(1)}, f32[256,256]{1,0:T(8,128)}, u32[]{:S(2)}) copy-start(f32[256,256]{1,0:T(8,128)} %reduce-scatter.5.cloned.1.call-done) | copy-start | bytes 786436
  473.3 206.8 %all-gather.7.cloned.1.call-start = ((), (), s32[]{:S(2)}) async-start(), calls=%async_computation.9 | async-start | bytes 2228224 | tf_op jit(solution)/shard_map/all_gather | solution.py:64
  648.8 197.3 %reduce-scatter.7.cloned.1.call-start = ((), (), s32[]{:S(2)}) async-start(), calls=%async_computation.10 | async-start | bytes 2359296 | tf_op jit(solution)/shard_map/reduce_scatter | solution.py:72
  773.0 121.1 %all-gather.11.cloned.1.call-start = ((), (), s32[]{:S(2)}) async-start(), calls=%async_computation.14 | async-start | bytes 1179648 | tf_op jit(solution)/shard_map/all_gather | solution.py:65
  773.8 267.5 %all-reduce.7.cloned.1.call-start = ((), (), s32[]{:S(2)}) async-start(), calls=%async_computation.13 | async-start | bytes 524288 | tf_op jit(solution)/shard_map/psum | solution.py:77
  848.4 260.3 %reduce-scatter.11.cloned.1.call-start = ((), (), s32[]{:S(2)}) async-start(), calls=%async_computation.15 | async-start | bytes 4456448 | tf_op jit(solution)/shard_map/reduce_scatter | solution.py:73
  1002.9 0.9 copy-start
  1002.9 40.2 %copy-start.6 = (f32[256,256]{1,0:T(8,128)S(1)}, f32[256,256]{1,0:T(8,128)}, u32[]{:S(2)}) copy-start(f32[256,256]{1,0:T(8,128)} %reduce-scatter.7.cloned.1.call-done) | copy-start | bytes 786436
Sparse Core Ops, SparseCore 0:
  37.5 112.1 all-gather.4
  242.5 74.2 reduce-scatter.4
  319.7 45.0 all-gather.8
  370.0 141.8 all-reduce.4
  514.1 65.1 reduce-scatter.8
  648.9 31.1 all-gather.6
  773.1 72.9 reduce-scatter.6
  849.0 45.0 all-gather.10
  899.4 141.8 all-reduce.6
  1043.5 65.1 reduce-scatter.10
where the time goes:
time: 1200 us; the launch traced here: 1190 us
  waiting for transfers between devices  576 us (48%)
  matrix products  327 us (27%)
  blocking collectives  156 us (13%)
  local copies, waits for them, and re-layouts  99.6 us (8%)
  between operations  14.8 us (1%)
    dot_general x16, matrix products, accumulate(): jnp.einsum('sn,sxp->nxp', onehot, contrib, precision=lax.Precision.HIGHEST)  200 us
    all_gather x2, waiting for transfers between devices, local(): right_cols = lax.all_gather(right_bf, 'row', axis=0, tiled=True)  144 us
    psum x2, blocking collectives, local(): lax.psum((jnp.sum(right_rest * right_rest, axis=0), jnp.sum(left_rest * l...  135 us
    reduce_scatter x2, waiting for transfers between devices, local(): lax.psum_scatter(right_part, 'col', scatter_dimension=0, tiled=True)  134 us
    reduce_scatter x2, waiting for transfers between devices, local(): lax.psum_scatter(left_part, 'row', scatter_dimension=0, tiled=True)  130 us
    dot_general x16, matrix products, accumulate(): jnp.einsum(form, group_tiles, picked, preferred_element_type=jnp.float32)  117 us
    all_gather x2, waiting for transfers between devices, local(): left_rows = lax.all_gather(left_bf, 'col', axis=0, tiled=True)  90.7 us
    psum x2, waiting for transfers between devices, local(): project = lax.psum(local_proj, ('row', 'col')) / order_rows  75.9 us
  transfers between devices with their start and end apart: 11, of which 10 were waited for; matrix products, arithmetic and copies ran while one was open for 20% of the time, Pallas kernels for 0%

commit v1 on v0

v1 whole, which is shorter than its diff:
```python
import functools

import jax
import jax.numpy as jnp
from jax import lax
from jax.experimental import pallas as pl
from jax.experimental.pallas import tpu as pltpu
from jax.sharding import PartitionSpec as P

ITERS = 2
epsilon = 1e-06
MESH = pl.DeviceIdType.MESH
F32 = jnp.float32
BF16 = jnp.bfloat16
HIGHEST = lax.Precision.HIGHEST


def span(index, size):
    return pl.ds(pl.multiple_of(index * size, size), size)


def krylov_kernel(
    nr, nc, order,
    slots_ref, tiles_hbm, right_ref, left_ref, diag_col, diag_row, scale_col, scale_row,
    v_out, w_out, h_out,
    tiles, ta, vg, wg, wt, r_new, lt_new,
    r_send, r_recv, sib_send, sib_recv, l_send, l_recv,
    h_loc, h_part, h_from_row, h_from_col, h_full,
    n_loc, n_part, n_from_row, n_from_col,
    tile_sem, v_ss, v_rs, f_ss, f_rs, w_ss, w_rs, r_ss, r_rs, s_ss, s_rs, l_ss, l_rs,
    h1_ss, h1_rs, h2_ss, h2_rs, h3_ss, h3_rs, n1_ss, n1_rs, n2_ss, n2_rs,
):
    row, col = lax.axis_index("row"), lax.axis_index("col")
    nq = nr // 2
    chip, core = row // 2, row % 2
    sibling = chip * 2 + (1 - core)
    tile = tiles.shape[1]
    block = 2 * tile
    slot_total = tiles_hbm.shape[0]
    h_rows = h_loc.shape[0] // nr

    def row_at(d):
        return lax.rem(row + d, nr)

    def col_at(d):
        return lax.rem(col + d, nc)

    def chip_at(d):
        return lax.rem(chip + d, nq) * 2 + core

    def each(low, high, body):
        def step(i, carry):
            body(i)
            return carry

        lax.fori_loop(low, high, step, 0)

    def remote(src, dst, send, recv, r, c):
        return pltpu.make_async_remote_copy(
            src_ref=src, dst_ref=dst, send_sem=send, recv_sem=recv,
            device_id=(r, c), device_id_type=MESH,
        )

    def v_copy(d, r):
        at = vg.at[span(r, block)]
        return remote(at, at, v_ss.at[d - 1], v_rs.at[d - 1], chip_at(d), col)

    def f_copy(e, r):
        at = vg.at[span(r, block)]
        return remote(at, at, f_ss.at[e], f_rs.at[e], sibling, col)

    def w_copy(d, c):
        return remote(wg.at[c], wg.at[c], w_ss.at[d - 1], w_rs.at[d - 1], row, col_at(d))

    def r_copy(d):
        return remote(r_send.at[d - 1], r_recv.at[d - 1], r_ss.at[d - 1], r_rs.at[d - 1], row, col_at(d))

    def s_copy(e):
        return remote(sib_send.at[e], sib_recv.at[e], s_ss.at[e], s_rs.at[e], sibling, col)

    def l_copy(d):
        return remote(l_send.at[d - 1], l_recv.at[d - 1], l_ss.at[d - 1], l_rs.at[d - 1], chip_at(d), col)

    def h1_copy(d, src, slot):
        return remote(
            h_loc.at[span(src, h_rows)], h_from_row.at[slot], h1_ss.at[d - 1], h1_rs.at[d - 1], row_at(d), col
        )

    def h2_copy(d, slot):
        return remote(h_part, h_from_col.at[slot], h2_ss.at[d - 1], h2_rs.at[d - 1], row, col_at(d))

    def h3_copy(d, slot):
        at = h_full.at[span(slot, h_rows)]
        return remote(at, at, h3_ss.at[d - 1], h3_rs.at[d - 1], row_at(d), col)

    def n1_copy(d, slot):
        return remote(n_loc, n_from_row.at[slot], n1_ss.at[d - 1], n1_rs.at[d - 1], row_at(d), col)

    def n2_copy(d, slot):
        return remote(n_part, n_from_col.at[slot], n2_ss.at[d - 1], n2_rs.at[d - 1], row, col_at(d))

    def row_behind(d):
        return lax.rem(row - d + nr, nr)

    def col_behind(d):
        return lax.rem(col - d + nc, nc)

    def chip_behind(d):
        return lax.rem(chip - d + nq, nq) * 2 + core

    load = pltpu.make_async_copy(tiles_hbm, tiles.at[pl.ds(0, slot_total)], tile_sem)
    load.start()

    barrier = pltpu.get_barrier_semaphore()
    each(1, nr, lambda d: pl.semaphore_signal(barrier, inc=1, device_id=(row_at(d), col), device_id_type=MESH))
    each(1, nc, lambda d: pl.semaphore_signal(barrier, inc=1, device_id=(row, col_at(d)), device_id_type=MESH))
    start_right = right_ref[...]
    v_out[...] = start_right
    wt[...] = jnp.transpose(start_right + left_ref[...])
    pl.semaphore_wait(barrier, nr + nc - 2)

    def assemble():
        load.wait()
        tiles[slot_total] = jnp.zeros((tile, tile), BF16)

        def one_row(a):
            for b in range(2 * nr):
                ta[span(a, tile), b * tile : (b + 1) * tile] = tiles[slots_ref[a * 2 * nr + b]]

        each(0, 2 * nc, one_row)

    def iteration(turn):
        vg[span(row, block)] = v_out[...].astype(BF16)
        each(1, nq, lambda d: v_copy(d, row).start())
        f_copy(0, row).start()
        scaled = scale_row[...] * wt[...]
        wg[col] = scaled.astype(BF16)
        each(1, nc, lambda d: w_copy(d, col).start())

        @pl.when(turn == 0)
        def _():
            assemble()

        def forward(d):
            v_copy(d, chip_behind(d)).wait_recv()
            f_copy(d, chip_behind(d)).start()

        each(1, nq, forward)

        def from_sibling(e):
            at = lax.rem(chip - e + nq, nq) * 2 + (1 - core)
            f_copy(e, at).wait_recv()

        each(0, nq, from_sibling)

        def right_part(c):
            return jnp.dot(ta[span(c, block)], vg[...], preferred_element_type=F32)

        def right_step(d):
            r_send[d - 1] = right_part(col_at(d)).astype(BF16)
            r_copy(d).start()

        each(1, nc, right_step)
        r_new[...] = right_part(col) + diag_col[...] * v_out[...]

        def v_sent(d):
            v_copy(d, row).wait_send()
            f_copy(d, row).wait_send()

        f_copy(0, row).wait_send()
        each(1, nq, v_sent)

        def right_sum(d):
            r_copy(d).wait_recv()
            r_new[...] += r_recv[d - 1].astype(F32)

        each(1, nc, right_sum)
        r_new[...] = scale_col[...] * r_new[...]

        h_loc[...] = jnp.dot(wt[...], r_new[...], precision=HIGHEST, preferred_element_type=F32)
        each(1, nr, lambda d: h1_copy(d, row_at(d), row).start())
        h_from_row[row] = h_loc[span(row, h_rows)]

        each(1, nc, lambda d: w_copy(d, col_behind(d)).wait_recv())

        def left_part(r):
            rows = jnp.concatenate([wg[c] for c in range(nc)], axis=1)
            return jnp.dot(rows, ta[:, span(r, block)], preferred_element_type=F32)

        def left_other(e):
            sib_send[e] = left_part(lax.rem(chip + e, nq) * 2 + (1 - core))
            s_copy(e).start()

        each(0, nq, left_other)

        each(1, nr, lambda d: h1_copy(d, row_at(d), row_behind(d)).wait_recv())
        part = h_from_row[0]
        for i in range(1, nr):
            part += h_from_row[i]
        h_part[...] = part
        each(1, nc, lambda d: h2_copy(d, col).start())
        h_from_col[col] = part

        def left_own(e):
            s_copy(e).wait_recv()
            l_send[e - 1] = (left_part(chip_at(e)) + sib_recv[e]).astype(BF16)
            l_copy(e).start()

        each(1, nq // 2, left_own)

        each(1, nc, lambda d: h2_copy(d, col_behind(d)).wait_recv())
        total = h_from_col[0]
        for i in range(1, nc):
            total += h_from_col[i]
        h_full[span(row, h_rows)] = total * (1.0 / order)
        each(1, nr, lambda d: h3_copy(d, row).start())

        each(nq // 2, nq, left_own)
        s_copy(0).wait_recv()
        scaled_again = scale_row[...] * wt[...]
        lt_new[...] = left_part(row) + sib_recv[0] + diag_row[...] * scaled_again

        each(1, nr, lambda d: h3_copy(d, row_behind(d)).wait_recv())
        project = h_full[...]
        h_out[turn] = project
        rest = r_new[...] - jnp.dot(v_out[...], project, precision=HIGHEST, preferred_element_type=F32)
        r_new[...] = rest
        n_loc[0:1] = jnp.sum(rest * rest, axis=0, keepdims=True)
        lt_new[...] -= jnp.dot(project, wt[...], precision=HIGHEST, preferred_element_type=F32)

        def left_sum(d):
            l_copy(d).wait_recv()
            lt_new[...] += l_recv[d - 1].astype(F32)

        each(1, nq, left_sum)
        left_rest = lt_new[...]
        n_loc[1:2] = jnp.sum(jnp.transpose(left_rest * left_rest), axis=0, keepdims=True)

        each(1, nc, lambda d: w_copy(d, col).wait_send())
        each(1, nc, lambda d: r_copy(d).wait_send())
        each(0, nq, lambda e: s_copy(e).wait_send())
        each(1, nq, lambda d: l_copy(d).wait_send())
        each(1, nr, lambda d: h1_copy(d, row_at(d), row).wait_send())
        each(1, nc, lambda d: h2_copy(d, col).wait_send())
        each(1, nr, lambda d: h3_copy(d, row).wait_send())

        each(1, nr, lambda d: n1_copy(d, row).start())
        n_from_row[row] = n_loc[...]
        each(1, nr, lambda d: n1_copy(d, row_behind(d)).wait_recv())
        sums = n_from_row[0]
        for i in range(1, nr):
            sums += n_from_row[i]
        n_part[...] = sums
        each(1, nc, lambda d: n2_copy(d, col).start())
        n_from_col[col] = sums
        each(1, nr, lambda d: n1_copy(d, row).wait_send())
        each(1, nc, lambda d: n2_copy(d, col_behind(d)).wait_recv())
        sums = n_from_col[0]
        for i in range(1, nc):
            sums += n_from_col[i]
        each(1, nc, lambda d: n2_copy(d, col).wait_send())
        norms = jnp.sqrt(sums * (1.0 / order) + epsilon)
        v_out[...] = r_new[...] / norms[0:1]
        ports = lt_new.shape[0]
        wt[...] = lt_new[...] / jnp.transpose(jnp.broadcast_to(norms[1:2], (lt_new.shape[1], ports)))

    n_loc[...] = jnp.zeros_like(n_loc)
    each(0, ITERS, iteration)
    w_out[...] = jnp.transpose(wt[...])


def local(tile_values, slot_codes, right_start, left_start, node_diagonal, row_scale):
    nr, nc = lax.axis_size("row"), lax.axis_size("col")
    slot_total, tile = tile_values.shape[:2]
    rows, ports = right_start.shape
    order = rows * nr * nc
    nq = nr // 2
    got_tiles = lax.all_to_all(tile_values, ("row", "col"), split_axis=0, concat_axis=0, tiled=True)
    got_codes = lax.all_to_all(slot_codes, ("row", "col"), split_axis=0, concat_axis=0, tiled=True)
    places = 4 * nr * nc
    hit = got_codes[None, :] == jnp.arange(places, dtype=jnp.int32)[:, None]
    slots = jnp.max(jnp.where(hit, jnp.arange(slot_total, dtype=jnp.int32)[None, :], -1), axis=1)
    slots = jnp.where(slots < 0, slot_total, slots)
    vmem = pl.BlockSpec(memory_space=pltpu.VMEM)
    sem = pltpu.SemaphoreType.DMA
    counts = (nq - 1, nq, nc - 1, nc - 1, nq, nq - 1, nr - 1, nc - 1, nr - 1, nr - 1, nc - 1)
    h_rows = ports // nr
    return pl.pallas_call(
        functools.partial(krylov_kernel, nr, nc, order),
        out_shape=(
            jax.ShapeDtypeStruct((rows, ports), F32),
            jax.ShapeDtypeStruct((rows, ports), F32),
            jax.ShapeDtypeStruct((ITERS, ports, ports), F32),
        ),
        in_specs=[
            pl.BlockSpec(memory_space=pltpu.SMEM),
            pl.BlockSpec(memory_space=pl.ANY),
            vmem, vmem, vmem, vmem, vmem, vmem,
        ],
        out_specs=(vmem, vmem, vmem),
        scratch_shapes=[
            pltpu.VMEM((slot_total + 1, tile, tile), BF16),
            pltpu.VMEM((2 * nc * tile, 2 * nr * tile), BF16),
            pltpu.VMEM((nr * rows, ports), BF16),
            pltpu.VMEM((nc, ports, rows), BF16),
            pltpu.VMEM((ports, rows), F32),
            pltpu.VMEM((rows, ports), F32),
            pltpu.VMEM((ports, rows), F32),
            pltpu.VMEM((nc - 1, rows, ports), BF16),
            pltpu.VMEM((nc - 1, rows, ports), BF16),
            pltpu.VMEM((nq, ports, rows), F32),
            pltpu.VMEM((nq, ports, rows), F32),
            pltpu.VMEM((nq - 1, ports, rows), BF16),
            pltpu.VMEM((nq - 1, ports, rows), BF16),
            pltpu.VMEM((ports, ports), F32),
            pltpu.VMEM((h_rows, ports), F32),
            pltpu.VMEM((nr, h_rows, ports), F32),
            pltpu.VMEM((nc, h_rows, ports), F32),
            pltpu.VMEM((ports, ports), F32),
            pltpu.VMEM((8, ports), F32),
            pltpu.VMEM((8, ports), F32),
            pltpu.VMEM((nr, 8, ports), F32),
            pltpu.VMEM((nc, 8, ports), F32),
            sem,
        ]
        + [sem((n,)) for n in counts for _ in range(2)],
        compiler_params=pltpu.CompilerParams(
            collective_id=0, has_side_effects=True, vmem_limit_bytes=58 * 2**20
        ),
        name="krylov",
    )(
        slots, got_tiles, right_start, left_start,
        node_diagonal[:, None], node_diagonal[None, :], row_scale[:, None], row_scale[None, :],
    )


def solution(mesh):
    return jax.shard_map(
        local,
        mesh=mesh,
        in_specs=(
            P(("row", "col"), None, None),
            P(("row", "col")),
            P(("row", "col"), None),
            P(("row", "col"), None),
            P(("row", "col")),
            P(("row", "col")),
        ),
        out_specs=(P(("row", "col"), None), P(("row", "col"), None), P()),
        check_vma=False,
    )
```

time: 1200 us -> 295 us (0.25); the launches traced: 1190 us -> 294 us
  waiting for transfers between devices: 576 us -> 96.2 us
  matrix products: 327 us -> 0 us
  Pallas kernels: 0 us -> 161 us
  blocking collectives: 156 us -> 21.1 us
  local copies, waits for them, and re-layouts: 99.6 us -> 8.27 us
  between operations: 14.8 us -> 0.68 us
    dot_general x38 -> x0, matrix products: 327 us -> none  [the longest x16 200 us: accumulate(): jnp.einsum('sn,sxp->nxp', onehot, contrib, precision=lax.Precision.HIGHEST)]
    reduce_scatter x4 -> x0, waiting for transfers between devices: 264 us -> none  [the longest x2 134 us: local(): lax.psum_scatter(right_part, 'col', scatter_dimension=0, tiled=True)]
    all_gather x4 -> x0, waiting for transfers between devices: 235 us -> none  [the longest x2 144 us: local(): right_cols = lax.all_gather(right_bf, 'row', axis=0, tiled=True)]
    pallas_call x0 -> x1, Pallas kernels: none -> 161 us  [local(): pl.pallas_call(functools.partial(krylov_kernel, nr, nc, order), out_shape...]
    psum x2 -> x0, blocking collectives: 135 us -> none  [local(): lax.psum((jnp.sum(right_rest * right_rest, axis=0), jnp.sum(left_rest * l...]
    all_to_all x1, waiting for transfers between devices: 0.01 us -> 96.2 us  [local(): lax.all_to_all(tile_values, ('row', 'col'), split_axis=0, concat_axis=0,...]
    psum x2 -> x0, waiting for transfers between devices: 75.9 us -> none  [local(): project = lax.psum(local_proj, ('row', 'col')) / order_rows]
    gather x16 -> x0, local copies, waits for them, and re-layouts: 66.8 us -> none  [accumulate(): picked = blocks[group_pick]]
  transfers between devices with their start and end apart: 11 -> 1, of which waited for: 10 -> 1; matrix products, arithmetic and copies ran while one was open for 20% -> 1% of each run, Pallas kernels for 0% -> 0%
where the time goes in v1:
time: 295 us; the launch traced here: 294 us
  Pallas kernels  161 us (55%)
  waiting for transfers between devices  96.2 us (33%)
  blocking collectives  21.1 us (7%)
  local copies, waits for them, and re-layouts  8.27 us (3%)
  starting transfers between devices  5.3 us (2%)
    pallas_call x1, Pallas kernels, local(): pl.pallas_call(functools.partial(krylov_kernel, nr, nc, order), out_shape...  161 us
    all_to_all x1, waiting for transfers between devices, local(): lax.all_to_all(tile_values, ('row', 'col'), split_axis=0, concat_axis=0,...  96.2 us
    all_to_all x1, blocking collectives, local(): lax.all_to_all(slot_codes, ('row', 'col'), split_axis=0, concat_axis=0, t...  21.1 us
  transfers between devices with their start and end apart: 1, of which 1 were waited for; matrix products, arithmetic and copies ran while one was open for 1% of the time, Pallas kernels for 0%

profile of v1, /device:TPU:1, one launch (start us, length us, event | category | flops | bytes accessed | tf_op | source)
XLA Modules:
  0.0 294.2 jit_solution(2183497987896003218)
XLA Ops:
  0.6 0.8 all_to_all.9
  1.4 21.1 %all_to_all.14 = s32[128,2,1]{1,2,0:T(1,128)S(1)} all-to-all(s32[128,2,1]{1,2,0:T(1,128)S(1)} %bitcast.6), channel_id=1, replica_groups=mesh['row'=16,'col'=8] {'row','col'}, dimensions={0} | all-to-all | bytes 2048 | tf_op jit(solution)/shard_map/all_to_all | solution.py:279
  22.6 0.0 copy-start.1
  22.6 0.0 copy-start
  22.6 5.3 %all-to-all-start.1 = ((bf16[256,128,128]{2,1,0:T(8,128)(2,1)}), bf16[256,128,128]{2,1,0:T(8,128)(2,1)}, u32[]{:S(2)}, u32[]{:S(2)}) async-start(bf16[256,128,128]{2,1,0:T(8,128)(2,1)} %param.6), calls=%async_computation.1 | async-start | bytes 16777216 | tf_op jit(solution)/shard_map/all_to_all | solution.py:278
  27.9 0.0 copy-done.1
  27.9 0.8 copy.16.scale_col
  28.7 0.0 copy-done
  28.7 0.8 copy.15.diag_col
  29.5 0.5 broadcast.3
  30.0 0.8 reduce.3
  30.8 0.1 eq.15
  31.0 0.2 select_reduce_fusion
  31.1 0.6 compare_select_fusion.slots_ref
  31.7 96.2 %all-to-all-done.1.tiles_hbm = bf16[256,128,128]{2,1,0:T(8,128)(2,1)} async-done(((bf16[256,128,128]{2,1,0:T(8,128)(2,1)}), bf16[256,128,128]{2,1,0:T(8,128)(2,1)}, u32[]{:S(2)}, u32[]{:S(2)}) %all-to-all-start.1) | async-done | bytes 8388640 | tf_op jit(solution)/shard_map/all_to_all | solution.py:278
  127.9 161.2 %krylov.1 = (f32[256,256]{1,0:T(8,128)}, f32[256,256]{1,0:T(8,128)}, f32[2,256,256]{2,1,0:T(8,128)}) custom-call(s32[512]{0:T(512)} %compare_select_fusion.slots_ref, bf16[256,128,128]{2,1,0:T(8,128)(2,1)} %all-to-all-done.1.tiles_hbm, f32[256,256]{1,0:T(8,128)} %right_ref.1, f32[256,256]{1,0:T(8,128)} %left_ref.1, f32[256,1]{1,0:T(8,128)} %copy.15.diag_col, ...), custom_call_target="tpu_custom_call" | custom-call | tf_op jit(solution)/shard_map/krylov/pallas_call | solution.py:288
  289.0 1.7 copy.20
  290.7 1.7 copy.21
  292.4 1.9 copy.22
Async XLA Ops:
  22.6 5.3 %copy-start.1 = (f32[256]{0:T(256)S(1)}, f32[256]{0:T(256)}, u32[]{:S(2)}) copy-start(f32[256]{0:T(256)} %param.11) | copy-start | bytes 3076
  22.6 6.1 %copy-start = (f32[256]{0:T(256)S(1)}, f32[256]{0:T(256)}, u32[]{:S(2)}) copy-start(f32[256]{0:T(256)} %param.10) | copy-start | bytes 3076
  22.6 105.3 %all-to-all-start.1 = ((bf16[256,128,128]{2,1,0:T(8,128)(2,1)}), bf16[256,128,128]{2,1,0:T(8,128)(2,1)}, u32[]{:S(2)}, u32[]{:S(2)}) async-start(bf16[256,128,128]{2,1,0:T(8,128)(2,1)} %param.6), calls=%async_computation.1 | async-start | bytes 16777216 | tf_op jit(solution)/shard_map/all_to_all | solution.py:278

commit v2 on v0

v2 whole, which is shorter than its diff:
```python
import functools

import jax
import jax.numpy as jnp
from jax import lax
from jax.experimental import pallas as pl
from jax.experimental.pallas import tpu as pltpu
from jax.sharding import PartitionSpec as P

ITERS = 2
epsilon = 1e-06
MESH = pl.DeviceIdType.MESH
F32 = jnp.float32
BF16 = jnp.bfloat16
HIGHEST = lax.Precision.HIGHEST


def span(index, size):
    return pl.ds(pl.multiple_of(index * size, size), size)


def each(low, high, body):
    def step(i, carry):
        body(i)
        return carry

    lax.fori_loop(low, high, step, 0)


def remote(src, dst, send, recv, to):
    return pltpu.make_async_remote_copy(
        src_ref=src, dst_ref=dst, send_sem=send, recv_sem=recv, device_id=to, device_id_type=MESH
    )


class Place:
    def __init__(self, nr, nc):
        self.nr, self.nc, self.nz, self.ny = nr, nc, nr // 4, nc // 2
        self.row, self.col = lax.axis_index("row"), lax.axis_index("col")
        self.z, self.xl, self.core = self.row // 4, (self.row // 2) % 2, self.row % 2
        self.xh, self.y = self.col // self.ny, self.col % self.ny

    def row_at(self, d):
        return lax.rem(self.row + d + self.nr, self.nr)

    def col_at(self, d):
        return lax.rem(self.col + d + self.nc, self.nc)

    def z_at(self, d):
        return lax.rem(self.z + d + self.nz, self.nz)

    def y_at(self, d):
        return lax.rem(self.y + d + self.ny, self.ny)

    def row_of(self, z, xl, core):
        return z * 4 + xl * 2 + core

    def col_of(self, xh, y):
        return xh * self.ny + y

    def greet(self):
        barrier = pltpu.get_barrier_semaphore()
        each(1, self.nr, lambda d: pl.semaphore_signal(
            barrier, inc=1, device_id=(self.row_at(d), self.col), device_id_type=MESH))
        each(1, self.nc, lambda d: pl.semaphore_signal(
            barrier, inc=1, device_id=(self.row, self.col_at(d)), device_id_type=MESH))
        return lambda: pl.semaphore_wait(barrier, self.nr + self.nc - 2)


class RightGather:
    def __init__(self, me, vg, block, sems):
        self.me, self.vg, self.block = me, vg, block
        self.x_ss, self.x_rs, self.z_ss, self.z_rs, self.f_ss, self.f_rs = sems

    def slot(self, r):
        return self.vg.at[span(r, self.block)]

    def x_copy(self, r):
        me = self.me
        return remote(self.slot(r), self.slot(r), self.x_ss, self.x_rs, (me.row_of(me.z, 1 - me.xl, me.core), me.col))

    def z_copy(self, second, d, r):
        me = self.me
        i = second * (me.nz - 1) + d - 1
        to = (me.row_of(me.z_at(d), me.xl, me.core), me.col)
        return remote(self.slot(r), self.slot(r), self.z_ss.at[i], self.z_rs.at[i], to)

    def f_copy(self, second, d, r):
        me = self.me
        i = second * me.nz + d
        to = (me.row_of(me.z, me.xl, 1 - me.core), me.col)
        return remote(self.slot(r), self.slot(r), self.f_ss.at[i], self.f_rs.at[i], to)

    def from_z(self, second, d, other=0):
        me = self.me
        xl = 1 - me.xl if second else me.xl
        core = 1 - me.core if other else me.core
        return me.row_of(me.z_at(-d), xl, core)

    def start(self):
        me = self.me
        self.x_copy(me.row).start()
        each(1, me.nz, lambda d: self.z_copy(0, d, me.row).start())
        self.f_copy(0, 0, me.row).start()

    def pass_x(self):
        r = self.from_z(1, 0)
        self.x_copy(r).wait_recv()
        each(1, self.me.nz, lambda d: self.z_copy(1, d, r).start())
        self.f_copy(1, 0, r).start()

    def pass_z(self):
        for second in range(2):
            def one(d, second=second):
                r = self.from_z(second, d)
                self.z_copy(second, d, r).wait_recv()
                self.f_copy(second, d, r).start()

            each(1, self.me.nz, one)

    def arrive(self):
        for second in range(2):
            each(0, self.me.nz, lambda d, second=second: self.f_copy(
                second, d, self.from_z(second, d, 1)).wait_recv())

    def sent(self):
        me = self.me
        self.x_copy(me.row).wait_send()
        for second in range(2):
            each(1, me.nz, lambda d, second=second: self.z_copy(second, d, me.row).wait_send())
            each(0, me.nz, lambda d, second=second: self.f_copy(second, d, me.row).wait_send())


class LeftGather:
    def __init__(self, me, wg, sems):
        self.me, self.wg = me, wg
        self.x_ss, self.x_rs, self.y_ss, self.y_rs = sems

    def x_copy(self, c):
        me = self.me
        return remote(self.wg.at[c], self.wg.at[c], self.x_ss, self.x_rs, (me.row, me.col_of(1 - me.xh, me.y)))

    def y_copy(self, second, d, c):
        me = self.me
        i = second * (me.ny - 1) + d - 1
        to = (me.row, me.col_of(me.xh, me.y_at(d)))
        return remote(self.wg.at[c], self.wg.at[c], self.y_ss.at[i], self.y_rs.at[i], to)

    def start(self):
        me = self.me
        self.x_copy(me.col).start()
        each(1, me.ny, lambda d: self.y_copy(0, d, me.col).start())

    def pass_x(self):
        me = self.me
        c = me.col_of(1 - me.xh, me.y)
        self.x_copy(c).wait_recv()
        each(1, me.ny, lambda d: self.y_copy(1, d, c).start())

    def arrive(self):
        me = self.me
        for second in range(2):
            xh = 1 - me.xh if second else me.xh
            each(1, me.ny, lambda d, second=second, xh=xh: self.y_copy(
                second, d, me.col_of(xh, me.y_at(-d))).wait_recv())

    def sent(self):
        me = self.me
        self.x_copy(me.col).wait_send()
        for second in range(2):
            each(1, me.ny, lambda d, second=second: self.y_copy(second, d, me.col).wait_send())


class Exchange:
    def __init__(self, me, along_row, src, slots, ss, rs, pick=None):
        self.me, self.along_row, self.src, self.slots, self.ss, self.rs = me, along_row, src, slots, ss, rs
        self.pick = pick or (lambda i: src)
        self.size = me.nr if along_row else me.nc
        self.mine = me.row if along_row else me.col

    def at(self, d):
        return self.me.row_at(d) if self.along_row else self.me.col_at(d)

    def copy(self, d, slot):
        me = self.me
        to = (self.at(d), me.col) if self.along_row else (me.row, self.at(d))
        return remote(self.pick(self.at(d)), self.slots.at[slot], self.ss.at[d - 1], self.rs.at[d - 1], to)

    def start(self):
        each(1, self.size, lambda d: self.copy(d, self.mine).start())

    def total(self):
        each(1, self.size, lambda d: self.copy(d, self.at(-d)).wait_recv())
        total = self.slots[0]
        for i in range(1, self.size):
            total += self.slots[i]
        return total

    def sent(self):
        each(1, self.size, lambda d: self.copy(d, self.mine).wait_send())


def gather_kernel(nr, nc, codes, right, left, scale_row, vg, wg, got, got_row, *sems):
    me = Place(nr, nc)
    hold = me.greet()
    block = right.shape[0]
    v = RightGather(me, vg, block, sems[:6])
    w = LeftGather(me, wg, sems[6:10])
    c1_ss, c1_rs, c2_ss, c2_rs = sems[10:14]
    start_right = right[...]
    vg[span(me.row, block)] = start_right.astype(BF16)
    wg[me.col] = (scale_row[...] * jnp.transpose(start_right + left[...])).astype(BF16)
    got_row[me.row] = codes[me.row]

    def c1_copy(d, slot):
        return remote(codes.at[me.row_at(d)], got_row.at[slot], c1_ss.at[d - 1], c1_rs.at[d - 1],
                      (me.row_at(d), me.col))

    def c2_copy(d, slot):
        return remote(got_row, got.at[slot], c2_ss.at[d - 1], c2_rs.at[d - 1], (me.row, me.col_at(d)))

    hold()
    each(1, nr, lambda d: c1_copy(d, me.row).start())
    each(1, nr, lambda d: c1_copy(d, me.row_at(-d)).wait_recv())
    each(1, nc, lambda d: c2_copy(d, me.col).start())
    v.start()
    w.start()
    got[me.col] = got_row[...]
    v.pass_x()
    w.pass_x()
    v.pass_z()
    each(1, nc, lambda d: c2_copy(d, me.col_at(-d)).wait_recv())
    w.arrive()
    v.arrive()
    v.sent()
    w.sent()
    each(1, nr, lambda d: c1_copy(d, me.row).wait_send())
    each(1, nc, lambda d: c2_copy(d, me.col).wait_send())


def krylov_kernel(
    nr, nc, order,
    slots_ref, tiles_hbm, vg_hbm, wg_hbm, right_ref, left_ref, diag_col, diag_row, scale_col, scale_row,
    r_new, lt_new, norm_out, h_out,
    tiles, ta, vg, wg, v_ref, wt,
    r_send, r_recv, sib_send, sib_recv, l_send, l_recv, l_keep, x_send, x_recv,
    h_loc, h_part, h_from_row, h_from_col, h_full,
    n_loc, n_part, n_from_row, n_from_col, m_loc, m_part, m_from_row, m_from_col,
    tile_sem, vg_sem, wg_sem, *sems,
):
    me = Place(nr, nc)
    row, col, nz = me.row, me.col, me.nz
    tile = tiles.shape[1]
    block = 2 * tile
    slot_total = tiles_hbm.shape[0]
    h_rows = h_loc.shape[0] // nr
    v = RightGather(me, vg, block, sems[:6])
    w = LeftGather(me, wg, sems[6:10])
    (r_ss, r_rs, s_ss, s_rs, l_ss, l_rs, x_ss, x_rs, h1_ss, h1_rs, h2_ss, h2_rs, h3_ss, h3_rs,
     n1_ss, n1_rs, n2_ss, n2_rs, m1_ss, m1_rs, m2_ss, m2_rs) = sems[10:]

    def r_copy(d):
        return remote(r_send.at[d - 1], r_recv.at[d - 1], r_ss.at[d - 1], r_rs.at[d - 1], (row, me.col_at(d)))

    def s_copy(e):
        to = (me.row_of(me.z, me.xl, 1 - me.core), col)
        return remote(sib_send.at[e], sib_recv.at[e], s_ss.at[e], s_rs.at[e], to)

    def l_copy(d):
        to = (me.row_of(me.z_at(d), me.xl, me.core), col)
        return remote(l_send.at[d - 1], l_recv.at[d - 1], l_ss.at[d - 1], l_rs.at[d - 1], to)

    def x_copy():
        return remote(x_send, x_recv, x_ss, x_rs, (me.row_of(me.z, 1 - me.xl, me.core), col))

    def h3_copy(d, slot):
        at = h_full.at[span(slot, h_rows)]
        return remote(at, at, h3_ss.at[d - 1], h3_rs.at[d - 1], (me.row_at(d), col))

    h1 = Exchange(me, True, h_loc, h_from_row, h1_ss, h1_rs, lambda i: h_loc.at[span(i, h_rows)])
    h2 = Exchange(me, False, h_part, h_from_col, h2_ss, h2_rs)
    n1 = Exchange(me, True, n_loc, n_from_row, n1_ss, n1_rs)
    n2 = Exchange(me, False, n_part, n_from_col, n2_ss, n2_rs)
    m1 = Exchange(me, True, m_loc, m_from_row, m1_ss, m1_rs)
    m2 = Exchange(me, False, m_part, m_from_col, m2_ss, m2_rs)

    load = pltpu.make_async_copy(tiles_hbm, tiles.at[pl.ds(0, slot_total)], tile_sem)
    load.start()
    load_vg = pltpu.make_async_copy(vg_hbm, vg, vg_sem)
    load_vg.start()
    load_wg = pltpu.make_async_copy(wg_hbm, wg, wg_sem)
    load_wg.start()
    hold = me.greet()
    wt[...] = jnp.transpose(right_ref[...] + left_ref[...])
    v_ref[...] = right_ref[...]
    n_loc[...] = jnp.zeros_like(n_loc)
    m_loc[...] = jnp.zeros_like(m_loc)
    tiles[slot_total] = jnp.zeros((tile, tile), BF16)
    load.wait()

    def one_row(a):
        for b in range(2 * nr):
            ta[span(a, tile), b * tile : (b + 1) * tile] = tiles[slots_ref[a * 2 * nr + b]]

    each(0, 2 * nc, one_row)
    load_vg.wait()
    load_wg.wait()
    hold()

    def right_part(c):
        return jnp.dot(ta[span(c, block)], vg[...], preferred_element_type=F32)

    def left_part(r):
        rows = jnp.concatenate([wg[c] for c in range(nc)], axis=1)
        return jnp.dot(rows, ta[:, span(r, block)], preferred_element_type=F32)

    def norm_of(total):
        return jnp.sqrt(total * (1.0 / order) + epsilon)

    for turn in range(ITERS):
        last = turn == ITERS - 1
        if turn:
            v.arrive()

        def right_step(d):
            r_send[d - 1] = right_part(me.col_at(d)).astype(BF16)
            r_copy(d).start()

        each(1, nc, right_step)
        r_new[...] = right_part(col) + diag_col[...] * v_ref[...]

        if turn:
            w.arrive()

        def left_other(e):
            sib_send[e] = left_part(me.row_of(me.z_at(e // 2), e % 2, 1 - me.core))
            s_copy(e).start()

        each(2, 2 * nz, left_other)
        each(0, 2, left_other)

        def left_own(e):
            s_copy(e).wait_recv()
            return left_part(me.row_of(me.z_at(e // 2), e % 2, me.core)) + sib_recv[e]

        def left_away(d):
            for i in range(2):
                l_send[d - 1, i] = left_own(2 * d + i).astype(BF16)
            l_copy(d).start()

        each(1, nz, left_away)

        def left_home(i):
            l_keep[i] = left_own(i)

        each(0, 2, left_home)

        def right_sum(d):
            r_copy(d).wait_recv()
            r_new[...] += r_recv[d - 1].astype(F32)

        each(1, nc, right_sum)
        r_new[...] = scale_col[...] * r_new[...]

        h_loc[...] = jnp.dot(wt[...], r_new[...], precision=HIGHEST, preferred_element_type=F32)
        h1.start()
        h_from_row[row] = h_loc[span(row, h_rows)]
        part = h1.total()
        h_part[...] = part
        h2.start()
        h_from_col[col] = part

        def left_sum(d):
            l_copy(d).wait_recv()
            for i in range(2):
                l_keep[i] += l_recv[d - 1, i].astype(F32)

        each(1, nz, left_sum)
        x_send[...] = l_keep[1 - me.xl]
        x_copy().start()

        h_full[span(row, h_rows)] = h2.total() * (1.0 / order)
        each(1, nr, lambda d: h3_copy(d, row).start())
        scaled = scale_row[...] * wt[...]
        lt_new[...] = l_keep[me.xl] + diag_row[...] * scaled
        each(1, nr, lambda d: h3_copy(d, me.row_at(-d)).wait_recv())

        project = h_full[...]
        rest = r_new[...] - jnp.dot(v_ref[...], project, precision=HIGHEST, preferred_element_type=F32)
        r_new[...] = rest
        n_loc[0:1] = jnp.sum(rest * rest, axis=0, keepdims=True)
        if not last:
            n1.start()
            n_from_row[row] = n_loc[...]

        h_out[turn] = h_full[...]
        lt_new[...] -= jnp.dot(h_full[...], wt[...], precision=HIGHEST, preferred_element_type=F32)
        x_copy().wait_recv()
        lt_new[...] += x_recv[...]
        left_rest = lt_new[...]
        left_norm = jnp.sum(jnp.transpose(left_rest * left_rest), axis=0, keepdims=True)
        if last:
            n_loc[1:2] = left_norm
            n1.start()
            n_from_row[row] = n_loc[...]
        else:
            m_loc[0:1] = left_norm
        n_part[...] = n1.total()
        n2.start()
        n_from_col[col] = n_part[...]

        if turn:
            v.sent()
            w.sent()
        each(1, nc, lambda d: r_copy(d).wait_send())
        each(0, 2 * nz, lambda e: s_copy(e).wait_send())
        each(1, nz, lambda d: l_copy(d).wait_send())
        x_copy().wait_send()
        h1.sent()
        h2.sent()
        each(1, nr, lambda d: h3_copy(d, row).wait_send())
        n1.sent()
        total = n2.total()
        n2.sent()
        if last:
            norm_out[...] = norm_of(total)
        else:
            v_new = r_new[...] / norm_of(total)[0:1]
            v_ref[...] = v_new
            vg[span(row, block)] = v_new.astype(BF16)
            v.start()
            m1.start()
            m_from_row[row] = m_loc[...]
            v.pass_x()
            m_part[...] = m1.total()
            m2.start()
            m_from_col[col] = m_part[...]
            m1.sent()
            norm = norm_of(m2.total())[0:1]
            m2.sent()
            size = lt_new.shape
            w_new = lt_new[...] / jnp.transpose(jnp.broadcast_to(norm, (size[1], size[0])))
            wt[...] = w_new
            wg[col] = (scale_row[...] * w_new).astype(BF16)
            w.start()
            v.pass_z()
            w.pass_x()


def finish_kernel(r_ref, lt_ref, norm_ref, h_ref, v_out, w_out, h_out):
    v_out[...] = r_ref[...] / norm_ref[0:1]
    w_out[...] = jnp.transpose(lt_ref[...]) / norm_ref[1:2]
    h_out[...] = h_ref[...]


def local(tile_values, slot_codes, right_start, left_start, node_diagonal, row_scale):
    nr, nc = lax.axis_size("row"), lax.axis_size("col")
    slot_total, tile = tile_values.shape[:2]
    rows, ports = right_start.shape
    order = rows * nr * nc
    nz, ny = nr // 4, nc // 2
    vmem = pl.BlockSpec(memory_space=pltpu.VMEM)
    any_space = pl.BlockSpec(memory_space=pl.ANY)
    sem = pltpu.SemaphoreType.DMA
    scale_row = row_scale[None, :]

    def pairs(*counts):
        return [sem((n,)) if n else sem for n in counts for _ in range(2)]

    gather_sems = pairs(0, 2 * (nz - 1), 2 * nz, 0, 2 * (ny - 1))

    got_tiles = lax.all_to_all(tile_values, ("row", "col"), split_axis=0, concat_axis=0, tiled=True)
    codes = jnp.pad(slot_codes.reshape(nr, 1, 2 * nc), ((0, 0), (0, 7), (0, 128 - 2 * nc)))
    vg, wg, got = pl.pallas_call(
        functools.partial(gather_kernel, nr, nc),
        out_shape=(
            jax.ShapeDtypeStruct((nr * rows, ports), BF16),
            jax.ShapeDtypeStruct((nc, ports, rows), BF16),
            jax.ShapeDtypeStruct((nc, nr, 8, 128), jnp.int32),
        ),
        in_specs=[vmem] * 4,
        out_specs=(vmem,) * 3,
        scratch_shapes=[pltpu.VMEM((nr, 8, 128), jnp.int32)] + gather_sems + pairs(nr - 1, nc - 1),
        compiler_params=pltpu.CompilerParams(
            collective_id=0, has_side_effects=True, vmem_limit_bytes=16 * 2**20
        ),
        cost_estimate=pl.CostEstimate(flops=10**10, bytes_accessed=10**7, transcendentals=0),
        name="gather",
    )(codes, right_start, left_start, scale_row)

    got = lax.dynamic_slice_in_dim(got[:, :, 0, :], 2 * lax.axis_index("col"), 2, axis=2)
    got_codes = jnp.transpose(got, (1, 0, 2)).reshape(slot_total)
    places = 4 * nr * nc
    hit = got_codes[None, :] == jnp.arange(places, dtype=jnp.int32)[:, None]
    slots = jnp.max(jnp.where(hit, jnp.arange(slot_total, dtype=jnp.int32)[None, :], -1), axis=1)
    slots = jnp.where(slots < 0, slot_total, slots)

    h_rows = ports // nr
    right_rest, left_rest, norms, projections = pl.pallas_call(
        functools.partial(krylov_kernel, nr, nc, order),
        out_shape=(
            jax.ShapeDtypeStruct((rows, ports), F32),
            jax.ShapeDtypeStruct((ports, rows), F32),
            jax.ShapeDtypeStruct((8, ports), F32),
            jax.ShapeDtypeStruct((ITERS, ports, ports), F32),
        ),
        in_specs=[pl.BlockSpec(memory_space=pltpu.SMEM)] + [any_space] * 3 + [vmem] * 6,
        out_specs=(vmem,) * 4,
        scratch_shapes=[
            pltpu.VMEM((slot_total + 1, tile, tile), BF16),
            pltpu.VMEM((2 * nc * tile, 2 * nr * tile), BF16),
            pltpu.VMEM((nr * rows, ports), BF16),
            pltpu.VMEM((nc, ports, rows), BF16),
            pltpu.VMEM((rows, ports), F32),
            pltpu.VMEM((ports, rows), F32),
            pltpu.VMEM((nc - 1, rows, ports), BF16),
            pltpu.VMEM((nc - 1, rows, ports), BF16),
            pltpu.VMEM((2 * nz, ports, rows), F32),
            pltpu.VMEM((2 * nz, ports, rows), F32),
            pltpu.VMEM((nz - 1, 2, ports, rows), BF16),
            pltpu.VMEM((nz - 1, 2, ports, rows), BF16),
            pltpu.VMEM((2, ports, rows), F32),
            pltpu.VMEM((ports, rows), F32),
            pltpu.VMEM((ports, rows), F32),
            pltpu.VMEM((ports, ports), F32),
            pltpu.VMEM((h_rows, ports), F32),
            pltpu.VMEM((nr, h_rows, ports), F32),
            pltpu.VMEM((nc, h_rows, ports), F32),
            pltpu.VMEM((ports, ports), F32),
        ]
        + [
            pltpu.VMEM((8, ports), F32),
            pltpu.VMEM((8, ports), F32),
            pltpu.VMEM((nr, 8, ports), F32),
            pltpu.VMEM((nc, 8, ports), F32),
        ]
        * 2
        + [sem] * 3
        + gather_sems
        + pairs(
            nc - 1, 2 * nz, nz - 1, 0, nr - 1, nc - 1, nr - 1, nr - 1, nc - 1, nr - 1, nc - 1
        ),
        compiler_params=pltpu.CompilerParams(
            collective_id=1, has_side_effects=True, vmem_limit_bytes=58 * 2**20
        ),
        name="krylov",
    )(
        slots, got_tiles, vg, wg, right_start, left_start,
        node_diagonal[:, None], node_diagonal[None, :], row_scale[:, None], scale_row,
    )
    return tuple(
        pl.pallas_call(
            finish_kernel,
            out_shape=(
                jax.ShapeDtypeStruct((rows, ports), F32),
                jax.ShapeDtypeStruct((rows, ports), F32),
                jax.ShapeDtypeStruct((ITERS, ports, ports), F32),
            ),
            in_specs=[vmem] * 4,
            out_specs=(vmem,) * 3,
            name="finish",
        )(right_rest, left_rest, norms, projections)
    )


def solution(mesh):
    return jax.shard_map(
        local,
        mesh=mesh,
        in_specs=(
            P(("row", "col"), None, None),
            P(("row", "col")),
            P(("row", "col"), None),
            P(("row", "col"), None),
            P(("row", "col")),
            P(("row", "col")),
        ),
        out_specs=(P(("row", "col"), None), P(("row", "col"), None), P()),
        check_vma=False,
    )
```

time: 1200 us -> 283 us (0.24); the launches traced: 1190 us -> 283 us
  waiting for transfers between devices: 576 us -> 0.01 us
  matrix products: 327 us -> 0 us
  Pallas kernels: 0 us -> 265 us
  blocking collectives: 156 us -> 0 us
  local copies, waits for them, and re-layouts: 99.6 us -> 4.47 us
  between operations: 14.8 us -> 0.75 us
    dot_general x38 -> x0, matrix products: 327 us -> none  [the longest x16 200 us: accumulate(): jnp.einsum('sn,sxp->nxp', onehot, contrib, precision=lax.Precision.HIGHEST)]
    pallas_call x0 -> x3, Pallas kernels: none -> 265 us  [the longest x1 140 us: local(): pl.pallas_call(functools.partial(krylov_kernel, nr, nc, order), out_shape...]
    reduce_scatter x4 -> x0, waiting for transfers between devices: 264 us -> none  [the longest x2 134 us: local(): lax.psum_scatter(right_part, 'col', scatter_dimension=0, tiled=True)]
    all_gather x4 -> x0, waiting for transfers between devices: 235 us -> none  [the longest x2 144 us: local(): right_cols = lax.all_gather(right_bf, 'row', axis=0, tiled=True)]
    psum x2 -> x0, blocking collectives: 135 us -> none  [local(): lax.psum((jnp.sum(right_rest * right_rest, axis=0), jnp.sum(left_rest * l...]
    psum x2 -> x0, waiting for transfers between devices: 75.9 us -> none  [local(): project = lax.psum(local_proj, ('row', 'col')) / order_rows]
    gather x16 -> x0, local copies, waits for them, and re-layouts: 66.8 us -> none  [accumulate(): picked = blocks[group_pick]]
    all_to_all x1 -> x0, blocking collectives: 21.1 us -> none  [local(): lax.all_to_all(slot_codes, ('row', 'col'), split_axis=0, concat_axis=0, t...]
  transfers between devices with their start and end apart: 11 -> 1, of which waited for: 10 -> 0; matrix products, arithmetic and copies ran while one was open for 20% -> 1% of each run, Pallas kernels for 0% -> 43%
where the time goes in v2:
time: 283 us
  Pallas kernels  265 us (94%)
  starting transfers between devices  12 us (4%)
  local copies, waits for them, and re-layouts  4.47 us (2%)
    pallas_call x1, Pallas kernels, local(): pl.pallas_call(functools.partial(krylov_kernel, nr, nc, order), out_shape...  140 us
    pallas_call x1, Pallas kernels, local(): pl.pallas_call(functools.partial(gather_kernel, nr, nc), out_shape=(jax.S...  123 us
    all_to_all x1, starting transfers between devices, local(): lax.all_to_all(tile_values, ('row', 'col'), split_axis=0, concat_axis=0,...  12 us
  transfers between devices with their start and end apart: 1, of which 0 were waited for; matrix products, arithmetic and copies ran while one was open for 1% of the time, Pallas kernels for 43%

profile of v2, /device:TPU:1, one launch (start us, length us, event | category | flops | bytes accessed | tf_op | source)
XLA Modules:
  0.0 283.3 jit_solution(1708229778547582985)
XLA Ops:
  0.6 0.0 copy-start.6
  0.6 0.0 copy-start.4
  0.7 0.0 copy-start.5
  0.7 0.0 copy-start.3
  0.7 0.0 copy-start.2
  0.7 12.0 %all-to-all-start = ((bf16[256,128,128]{2,1,0:T(8,128)(2,1)}), bf16[256,128,128]{2,1,0:T(8,128)(2,1)}, u32[]{:S(2)}, u32[]{:S(2)}) async-start(bf16[256,128,128]{2,1,0:T(8,128)(2,1)} %param.6), calls=%async_computation | async-start | bytes 16777216 | tf_op jit(solution)/shard_map/all_to_all | solution.py:472
  12.7 0.0 copy-done.6
  12.7 0.1 reshape.11
  12.8 0.0 copy-done.4
  12.8 0.8 copy.18.scale_col
  13.6 0.0 copy-done.5
  13.6 0.8 copy.17.diag_col
  14.4 0.0 copy-done.3
  14.4 0.0 copy-done.2
  14.4 122.9 %gather.1 = (bf16[4096,256]{1,0:T(8,128)(2,1)S(1)}, bf16[8,256,256]{2,1,0:T(8,128)(2,1)S(1)}, s32[8,16,8,128]{3,2,1,0:T(8,128)S(1)}) custom-call(s32[16,8,128]{2,1,0:T(8,128)S(1)} %pad.4.codes, f32[256,256]{1,0:T(8,128)S(1)} %copy-done.2, f32[256,256]{1,0:T(8,128)S(1)} %copy-done.3, f32[1,256]{1,0:T(1,128)S(1)} %bitcast.11), custom_call_target="tpu_custom_call" | custom-call | flops 10000000000 | bytes 10000000 | tf_op jit(solution)/shard_map/gather/pallas_call | solution.py:474
  137.3 1.4 copy-done
  138.7 1.0 copy-done.1
  139.7 0.2 constant_dynamic-slice_fusion
  139.9 0.1 eq.15
  140.1 0.2 select_reduce_fusion
  140.2 0.6 compare_select_fusion.slots_ref
  140.8 0.0 all-to-all-done.tiles_hbm
  140.8 140.2 %krylov.1 = (f32[256,256]{1,0:T(8,128)}, f32[256,256]{1,0:T(8,128)}, f32[8,256]{1,0:T(8,128)}, f32[2,256,256]{2,1,0:T(8,128)}) custom-call(s32[512]{0:T(512)} %compare_select_fusion.slots_ref, bf16[256,128,128]{2,1,0:T(8,128)(2,1)} %all-to-all-done.tiles_hbm, bf16[4096,256]{1,0:T(8,128)(2,1)} %copy-done, bf16[8,256,256]{2,1,0:T(8,128)(2,1)} %copy-done.1, ...), custom_call_target="tpu_custom_call" | custom-call | tf_op jit(solution)/shard_map/krylov/pallas_call | solution.py:499
  281.0 2.3 finish.1
  (5 shorter events, 0.1 us)
Async XLA Ops:
  0.6 12.0 %copy-start.6 = (s32[256]{0:T(256)S(1)}, s32[256]{0:T(256)}, u32[]{:S(2)}) copy-start(s32[256]{0:T(256)} %param.7) | copy-start | bytes 3076
  0.6 12.1 %copy-start.4 = (f32[256]{0:T(256)S(1)}, f32[256]{0:T(256)}, u32[]{:S(2)}) copy-start(f32[256]{0:T(256)} %param.11) | copy-start | bytes 3076
  0.7 12.9 %copy-start.5 = (f32[256]{0:T(256)S(1)}, f32[256]{0:T(256)}, u32[]{:S(2)}) copy-start(f32[256]{0:T(256)} %param.10) | copy-start | bytes 3076
  0.7 13.7 %copy-start.3 = (f32[256,256]{1,0:T(8,128)S(1)}, f32[256,256]{1,0:T(8,128)}, u32[]{:S(2)}) copy-start(f32[256,256]{1,0:T(8,128)} %left_ref.1) | copy-start | bytes 786436
  0.7 13.7 %copy-start.2 = (f32[256,256]{1,0:T(8,128)S(1)}, f32[256,256]{1,0:T(8,128)}, u32[]{:S(2)}) copy-start(f32[256,256]{1,0:T(8,128)} %right_ref.1) | copy-start | bytes 786436
  0.7 140.1 %all-to-all-start = ((bf16[256,128,128]{2,1,0:T(8,128)(2,1)}), bf16[256,128,128]{2,1,0:T(8,128)(2,1)}, u32[]{:S(2)}, u32[]{:S(2)}) async-start(bf16[256,128,128]{2,1,0:T(8,128)(2,1)} %param.6), calls=%async_computation | async-start | bytes 16777216 | tf_op jit(solution)/shard_map/all_to_all | solution.py:472
  137.3 1.4 copy-start
  138.7 1.0 copy-start.1

commit v3 on v2

--- a/solution.py
+++ b/solution.py
@@ -221,10 +221,10 @@
 
     hold()
     each(1, nr, lambda d: c1_copy(d, me.row).start())
+    v.start()
+    w.start()
     each(1, nr, lambda d: c1_copy(d, me.row_at(-d)).wait_recv())
     each(1, nc, lambda d: c2_copy(d, me.col).start())
-    v.start()
-    w.start()
     got[me.col] = got_row[...]
     v.pass_x()
     w.pass_x()
@@ -245,7 +245,7 @@
     tiles, ta, vg, wg, v_ref, wt,
     r_send, r_recv, sib_send, sib_recv, l_send, l_recv, l_keep, x_send, x_recv,
     h_loc, h_part, h_from_row, h_from_col, h_full,
-    n_loc, n_part, n_from_row, n_from_col, m_loc, m_part, m_from_row, m_from_col,
+    n_loc, n_part, n_from_row, n_from_col,
     tile_sem, vg_sem, wg_sem, *sems,
 ):
     me = Place(nr, nc)
@@ -253,11 +253,11 @@
     tile = tiles.shape[1]
     block = 2 * tile
     slot_total = tiles_hbm.shape[0]
-    h_rows = h_loc.shape[0] // nr
+    h_rows = h_loc.shape[0] // nc
     v = RightGather(me, vg, block, sems[:6])
     w = LeftGather(me, wg, sems[6:10])
     (r_ss, r_rs, s_ss, s_rs, l_ss, l_rs, x_ss, x_rs, h1_ss, h1_rs, h2_ss, h2_rs, h3_ss, h3_rs,
-     n1_ss, n1_rs, n2_ss, n2_rs, m1_ss, m1_rs, m2_ss, m2_rs) = sems[10:]
+     n1_ss, n1_rs, n2_ss, n2_rs) = sems[10:]
 
     def r_copy(d):
         return remote(r_send.at[d - 1], r_recv.at[d - 1], r_ss.at[d - 1], r_rs.at[d - 1], (row, me.col_at(d)))
@@ -266,23 +266,21 @@
         to = (me.row_of(me.z, me.xl, 1 - me.core), col)
         return remote(sib_send.at[e], sib_recv.at[e], s_ss.at[e], s_rs.at[e], to)
 
-    def l_copy(d):
-        to = (me.row_of(me.z_at(d), me.xl, me.core), col)
-        return remote(l_send.at[d - 1], l_recv.at[d - 1], l_ss.at[d - 1], l_rs.at[d - 1], to)
+    def l_copy(i):
+        to = (me.row_of(me.z_at(i % (nz - 1) + 1), me.xl, me.core), col)
+        return remote(l_send.at[i], l_recv.at[i], l_ss.at[i], l_rs.at[i], to)
 
     def x_copy():
         return remote(x_send, x_recv, x_ss, x_rs, (me.row_of(me.z, 1 - me.xl, me.core), col))
 
     def h3_copy(d, slot):
         at = h_full.at[span(slot, h_rows)]
-        return remote(at, at, h3_ss.at[d - 1], h3_rs.at[d - 1], (me.row_at(d), col))
-
-    h1 = Exchange(me, True, h_loc, h_from_row, h1_ss, h1_rs, lambda i: h_loc.at[span(i, h_rows)])
-    h2 = Exchange(me, False, h_part, h_from_col, h2_ss, h2_rs)
+        return remote(at, at, h3_ss.at[d - 1], h3_rs.at[d - 1], (row, me.col_at(d)))
+
+    h1 = Exchange(me, False, h_loc, h_from_col, h1_ss, h1_rs, lambda i: h_loc.at[span(i, h_rows)])
+    h2 = Exchange(me, True, h_part, h_from_row, h2_ss, h2_rs)
     n1 = Exchange(me, True, n_loc, n_from_row, n1_ss, n1_rs)
     n2 = Exchange(me, False, n_part, n_from_col, n2_ss, n2_rs)
-    m1 = Exchange(me, True, m_loc, m_from_row, m1_ss, m1_rs)
-    m2 = Exchange(me, False, m_part, m_from_col, m2_ss, m2_rs)
 
     load = pltpu.make_async_copy(tiles_hbm, tiles.at[pl.ds(0, slot_total)], tile_sem)
     load.start()
@@ -294,7 +292,6 @@
     wt[...] = jnp.transpose(right_ref[...] + left_ref[...])
     v_ref[...] = right_ref[...]
     n_loc[...] = jnp.zeros_like(n_loc)
-    m_loc[...] = jnp.zeros_like(m_loc)
     tiles[slot_total] = jnp.zeros((tile, tile), BF16)
     load.wait()
 
@@ -314,6 +311,9 @@
         rows = jnp.concatenate([wg[c] for c in range(nc)], axis=1)
         return jnp.dot(rows, ta[:, span(r, block)], preferred_element_type=F32)
 
+    def xl_of(home):
+        return me.xl * home + (1 - me.xl) * (1 - home)
+
     def norm_of(total):
         return jnp.sqrt(total * (1.0 / order) + epsilon)
 
@@ -333,27 +333,23 @@
             w.arrive()
 
         def left_other(e):
-            sib_send[e] = left_part(me.row_of(me.z_at(e // 2), e % 2, 1 - me.core))
+            sib_send[e] = left_part(me.row_of(me.z_at(e % nz + 1), xl_of(e // nz), 1 - me.core))
             s_copy(e).start()
-
-        each(2, 2 * nz, left_other)
-        each(0, 2, left_other)
 
         def left_own(e):
             s_copy(e).wait_recv()
-            return left_part(me.row_of(me.z_at(e // 2), e % 2, me.core)) + sib_recv[e]
-
-        def left_away(d):
-            for i in range(2):
-                l_send[d - 1, i] = left_own(2 * d + i).astype(BF16)
-            l_copy(d).start()
-
-        each(1, nz, left_away)
-
-        def left_home(i):
-            l_keep[i] = left_own(i)
-
-        each(0, 2, left_home)
+            return left_part(me.row_of(me.z_at(e % nz + 1), xl_of(e // nz), me.core)) + sib_recv[e]
+
+        for home in range(2):
+            each(home * nz, home * nz + nz, left_other)
+
+            def left_away(d, home=home):
+                i = home * (nz - 1) + d
+                l_send[i] = left_own(home * nz + d).astype(BF16)
+                l_copy(i).start()
+
+            each(0, nz - 1, left_away)
+            l_keep[home] = left_own(home * nz + nz - 1)
 
         def right_sum(d):
             r_copy(d).wait_recv()
@@ -364,47 +360,44 @@
 
         h_loc[...] = jnp.dot(wt[...], r_new[...], precision=HIGHEST, preferred_element_type=F32)
         h1.start()
-        h_from_row[row] = h_loc[span(row, h_rows)]
+        h_from_col[col] = h_loc[span(col, h_rows)]
         part = h1.total()
         h_part[...] = part
         h2.start()
-        h_from_col[col] = part
-
-        def left_sum(d):
-            l_copy(d).wait_recv()
-            for i in range(2):
-                l_keep[i] += l_recv[d - 1, i].astype(F32)
-
-        each(1, nz, left_sum)
-        x_send[...] = l_keep[1 - me.xl]
+        h_from_row[row] = part
+
+        def left_sum(home):
+            def one(d):
+                i = home * (nz - 1) + d
+                l_copy(i).wait_recv()
+                l_keep[home] += l_recv[i].astype(F32)
+
+            each(0, nz - 1, one)
+
+        left_sum(0)
+        x_send[...] = l_keep[0]
         x_copy().start()
 
-        h_full[span(row, h_rows)] = h2.total() * (1.0 / order)
-        each(1, nr, lambda d: h3_copy(d, row).start())
+        h_full[span(col, h_rows)] = h2.total() * (1.0 / order)
+        each(1, nc, lambda d: h3_copy(d, col).start())
         scaled = scale_row[...] * wt[...]
-        lt_new[...] = l_keep[me.xl] + diag_row[...] * scaled
-        each(1, nr, lambda d: h3_copy(d, me.row_at(-d)).wait_recv())
+        left_sum(1)
+        lt_new[...] = l_keep[1] + diag_row[...] * scaled
+        each(1, nc, lambda d: h3_copy(d, me.col_at(-d)).wait_recv())
 
         project = h_full[...]
         rest = r_new[...] - jnp.dot(v_ref[...], project, precision=HIGHEST, preferred_element_type=F32)
         r_new[...] = rest
         n_loc[0:1] = jnp.sum(rest * rest, axis=0, keepdims=True)
-        if not last:
-            n1.start()
-            n_from_row[row] = n_loc[...]
 
         h_out[turn] = h_full[...]
         lt_new[...] -= jnp.dot(h_full[...], wt[...], precision=HIGHEST, preferred_element_type=F32)
         x_copy().wait_recv()
         lt_new[...] += x_recv[...]
         left_rest = lt_new[...]
-        left_norm = jnp.sum(jnp.transpose(left_rest * left_rest), axis=0, keepdims=True)
-        if last:
-            n_loc[1:2] = left_norm
-            n1.start()
-            n_from_row[row] = n_loc[...]
-        else:
-            m_loc[0:1] = left_norm
+        n_loc[1:2] = jnp.sum(jnp.transpose(left_rest * left_rest), axis=0, keepdims=True)
+        n1.start()
+        n_from_row[row] = n_loc[...]
         n_part[...] = n1.total()
         n2.start()
         n_from_col[col] = n_part[...]
@@ -414,37 +407,30 @@
             w.sent()
         each(1, nc, lambda d: r_copy(d).wait_send())
         each(0, 2 * nz, lambda e: s_copy(e).wait_send())
-        each(1, nz, lambda d: l_copy(d).wait_send())
+        each(0, 2 * (nz - 1), lambda i: l_copy(i).wait_send())
         x_copy().wait_send()
         h1.sent()
         h2.sent()
-        each(1, nr, lambda d: h3_copy(d, row).wait_send())
+        each(1, nc, lambda d: h3_copy(d, col).wait_send())
         n1.sent()
         total = n2.total()
         n2.sent()
+        norms = norm_of(total)
         if last:
-            norm_out[...] = norm_of(total)
+            norm_out[...] = norms
         else:
-            v_new = r_new[...] / norm_of(total)[0:1]
+            v_new = r_new[...] / norms[0:1]
             v_ref[...] = v_new
             vg[span(row, block)] = v_new.astype(BF16)
             v.start()
-            m1.start()
-            m_from_row[row] = m_loc[...]
-            v.pass_x()
-            m_part[...] = m1.total()
-            m2.start()
-            m_from_col[col] = m_part[...]
-            m1.sent()
-            norm = norm_of(m2.total())[0:1]
-            m2.sent()
             size = lt_new.shape
-            w_new = lt_new[...] / jnp.transpose(jnp.broadcast_to(norm, (size[1], size[0])))
+            w_new = lt_new[...] / jnp.transpose(jnp.broadcast_to(norms[1:2], (size[1], size[0])))
             wt[...] = w_new
             wg[col] = (scale_row[...] * w_new).astype(BF16)
             w.start()
+            v.pass_x()
+            w.pass_x()
             v.pass_z()
-            w.pass_x()
 
 
 def finish_kernel(r_ref, lt_ref, norm_ref, h_ref, v_out, w_out, h_out):
@@ -495,7 +481,7 @@
     slots = jnp.max(jnp.where(hit, jnp.arange(slot_total, dtype=jnp.int32)[None, :], -1), axis=1)
     slots = jnp.where(slots < 0, slot_total, slots)
 
-    h_rows = ports // nr
+    h_rows = ports // nc
     right_rest, left_rest, norms, projections = pl.pallas_call(
         functools.partial(krylov_kernel, nr, nc, order),
         out_shape=(
@@ -517,8 +503,8 @@
             pltpu.VMEM((nc - 1, rows, ports), BF16),
             pltpu.VMEM((2 * nz, ports, rows), F32),
             pltpu.VMEM((2 * nz, ports, rows), F32),
-            pltpu.VMEM((nz - 1, 2, ports, rows), BF16),
-            pltpu.VMEM((nz - 1, 2, ports, rows), BF16),
+            pltpu.VMEM((2 * (nz - 1), ports, rows), BF16),
+            pltpu.VMEM((2 * (nz - 1), ports, rows), BF16),
             pltpu.VMEM((2, ports, rows), F32),
             pltpu.VMEM((ports, rows), F32),
             pltpu.VMEM((ports, rows), F32),
@@ -527,18 +513,15 @@
             pltpu.VMEM((nr, h_rows, ports), F32),
             pltpu.VMEM((nc, h_rows, ports), F32),
             pltpu.VMEM((ports, ports), F32),
-        ]
-        + [
             pltpu.VMEM((8, ports), F32),
             pltpu.VMEM((8, ports), F32),
             pltpu.VMEM((nr, 8, ports), F32),
             pltpu.VMEM((nc, 8, ports), F32),
         ]
-        * 2
         + [sem] * 3
         + gather_sems
         + pairs(
-            nc - 1, 2 * nz, nz - 1, 0, nr - 1, nc - 1, nr - 1, nr - 1, nc - 1, nr - 1, nc - 1
+            nc - 1, 2 * nz, 2 * (nz - 1), 0, nc - 1, nr - 1, nc - 1, nr - 1, nc - 1
         ),
         compiler_params=pltpu.CompilerParams(
             collective_id=1, has_side_effects=True, vmem_limit_bytes=58 * 2**20

time: 283 us -> 269 us (0.951)
  Pallas kernels: 265 us -> 251 us
    pallas_call x1, Pallas kernels: 140 us -> 131 us  [local(): pl.pallas_call(functools.partial(krylov_kernel, nr, nc, order), out_shape...]
    pallas_call x1, Pallas kernels: 123 us -> 118 us  [local(): pl.pallas_call(functools.partial(gather_kernel, nr, nc), out_shape=(jax.S...]
  transfers between devices with their start and end apart: 1 -> 1, of which waited for: 0 -> 0; matrix products, arithmetic and copies ran while one was open for 1% -> 1% of each run, Pallas kernels for 43% -> 44%
where the time goes in v3:
time: 269 us
  Pallas kernels  251 us (93%)
  starting transfers between devices  12 us (4%)
  local copies, waits for them, and re-layouts  4.47 us (2%)
    pallas_call x1, Pallas kernels, local(): pl.pallas_call(functools.partial(krylov_kernel, nr, nc, order), out_shape...  131 us
    pallas_call x1, Pallas kernels, local(): pl.pallas_call(functools.partial(gather_kernel, nr, nc), out_shape=(jax.S...  118 us
    all_to_all x1, starting transfers between devices, local(): lax.all_to_all(tile_values, ('row', 'col'), split_axis=0, concat_axis=0,...  12 us
  transfers between devices with their start and end apart: 1, of which 0 were waited for; matrix products, arithmetic and copies ran while one was open for 1% of the time, Pallas kernels for 44%

profile of v3, /device:TPU:1, one launch (start us, length us, event | category | flops | bytes accessed | tf_op | source)
XLA Modules:
  0.0 269.1 jit_solution(4659605064559766589)
XLA Ops:
  0.6 0.0 copy-start.6
  0.6 0.0 copy-start.4
  0.7 0.0 copy-start.5
  0.7 0.0 copy-start.3
  0.7 0.0 copy-start.2
  0.7 12.0 %all-to-all-start = ((bf16[256,128,128]{2,1,0:T(8,128)(2,1)}), bf16[256,128,128]{2,1,0:T(8,128)(2,1)}, u32[]{:S(2)}, u32[]{:S(2)}) async-start(bf16[256,128,128]{2,1,0:T(8,128)(2,1)} %param.6), calls=%async_computation | async-start | bytes 16777216 | tf_op jit(solution)/shard_map/all_to_all | solution.py:458
  12.7 0.0 copy-done.6
  12.7 0.1 reshape.11
  12.8 0.0 copy-done.4
  12.8 0.8 copy.18.scale_col
  13.6 0.0 copy-done.5
  13.6 0.8 copy.17.diag_col
  14.4 0.0 copy-done.3
  14.4 0.0 copy-done.2
  14.4 118.4 %gather.1 = (bf16[4096,256]{1,0:T(8,128)(2,1)S(1)}, bf16[8,256,256]{2,1,0:T(8,128)(2,1)S(1)}, s32[8,16,8,128]{3,2,1,0:T(8,128)S(1)}) custom-call(s32[16,8,128]{2,1,0:T(8,128)S(1)} %pad.4.codes, f32[256,256]{1,0:T(8,128)S(1)} %copy-done.2, f32[256,256]{1,0:T(8,128)S(1)} %copy-done.3, f32[1,256]{1,0:T(1,128)S(1)} %bitcast.11), custom_call_target="tpu_custom_call" | custom-call | flops 10000000000 | bytes 10000000 | tf_op jit(solution)/shard_map/gather/pallas_call | solution.py:460
  132.8 1.4 copy-done
  134.2 1.0 copy-done.1
  135.2 0.2 constant_dynamic-slice_fusion
  135.5 0.1 eq.15
  135.6 0.2 select_reduce_fusion
  135.8 0.6 compare_select_fusion.slots_ref
  136.3 0.0 all-to-all-done.tiles_hbm
  136.3 130.5 %krylov.1 = (f32[256,256]{1,0:T(8,128)}, f32[256,256]{1,0:T(8,128)}, f32[8,256]{1,0:T(8,128)}, f32[2,256,256]{2,1,0:T(8,128)}) custom-call(s32[512]{0:T(512)} %compare_select_fusion.slots_ref, bf16[256,128,128]{2,1,0:T(8,128)(2,1)} %all-to-all-done.tiles_hbm, bf16[4096,256]{1,0:T(8,128)(2,1)} %copy-done, bf16[8,256,256]{2,1,0:T(8,128)(2,1)} %copy-done.1, ...), custom_call_target="tpu_custom_call" | custom-call | tf_op jit(solution)/shard_map/krylov/pallas_call | solution.py:485
  266.9 2.3 finish.1
  (5 shorter events, 0.1 us)
Async XLA Ops:
  0.6 12.0 %copy-start.6 = (s32[256]{0:T(256)S(1)}, s32[256]{0:T(256)}, u32[]{:S(2)}) copy-start(s32[256]{0:T(256)} %param.7) | copy-start | bytes 3076
  0.6 12.1 %copy-start.4 = (f32[256]{0:T(256)S(1)}, f32[256]{0:T(256)}, u32[]{:S(2)}) copy-start(f32[256]{0:T(256)} %param.11) | copy-start | bytes 3076
  0.7 12.9 %copy-start.5 = (f32[256]{0:T(256)S(1)}, f32[256]{0:T(256)}, u32[]{:S(2)}) copy-start(f32[256]{0:T(256)} %param.10) | copy-start | bytes 3076
  0.7 13.7 %copy-start.3 = (f32[256,256]{1,0:T(8,128)S(1)}, f32[256,256]{1,0:T(8,128)}, u32[]{:S(2)}) copy-start(f32[256,256]{1,0:T(8,128)} %left_ref.1) | copy-start | bytes 786436
  0.7 13.7 %copy-start.2 = (f32[256,256]{1,0:T(8,128)S(1)}, f32[256,256]{1,0:T(8,128)}, u32[]{:S(2)}) copy-start(f32[256,256]{1,0:T(8,128)} %right_ref.1) | copy-start | bytes 786436
  0.7 135.7 %all-to-all-start = ((bf16[256,128,128]{2,1,0:T(8,128)(2,1)}), bf16[256,128,128]{2,1,0:T(8,128)(2,1)}, u32[]{:S(2)}, u32[]{:S(2)}) async-start(bf16[256,128,128]{2,1,0:T(8,128)(2,1)} %param.6), calls=%async_computation | async-start | bytes 16777216 | tf_op jit(solution)/shard_map/all_to_all | solution.py:458
  132.8 1.4 copy-start
  134.2 1.0 copy-start.1

commit v4 on v3

--- a/solution.py
+++ b/solution.py
@@ -19,12 +19,12 @@
     return pl.ds(pl.multiple_of(index * size, size), size)
 
 
-def each(low, high, body):
+def each(low, high, body, unroll=False):
     def step(i, carry):
         body(i)
         return carry
 
-    lax.fori_loop(low, high, step, 0)
+    lax.fori_loop(low, high, step, 0, unroll=unroll)
 
 
 def remote(src, dst, send, recv, to):
@@ -83,52 +83,46 @@
         me = self.me
         i = second * (me.nz - 1) + d - 1
         to = (me.row_of(me.z_at(d), me.xl, me.core), me.col)
-        return remote(self.slot(r), self.slot(r), self.z_ss.at[i], self.z_rs.at[i], to)
-
-    def f_copy(self, second, d, r):
-        me = self.me
-        i = second * me.nz + d
-        to = (me.row_of(me.z, me.xl, 1 - me.core), me.col)
-        return remote(self.slot(r), self.slot(r), self.f_ss.at[i], self.f_rs.at[i], to)
-
-    def from_z(self, second, d, other=0):
-        me = self.me
-        xl = 1 - me.xl if second else me.xl
-        core = 1 - me.core if other else me.core
-        return me.row_of(me.z_at(-d), xl, core)
+        return remote(self.slot(r), self.slot(r), self.z_ss, self.z_rs.at[i], to)
+
+    def f_copy(self, second, r, blocks=0):
+        me = self.me
+        at = self.vg.at[pl.ds(0, blocks * self.block)] if blocks else self.slot(r)
+        return remote(at, at, self.f_ss, self.f_rs.at[second], (me.row_of(me.z, me.xl, 1 - me.core), me.col))
+
+    def from_z(self, second, d):
+        me = self.me
+        return me.row_of(me.z_at(-d), 1 - me.xl if second else me.xl, me.core)
 
     def start(self):
         me = self.me
         self.x_copy(me.row).start()
         each(1, me.nz, lambda d: self.z_copy(0, d, me.row).start())
-        self.f_copy(0, 0, me.row).start()
+        self.f_copy(0, me.row).start()
 
     def pass_x(self):
         r = self.from_z(1, 0)
         self.x_copy(r).wait_recv()
         each(1, self.me.nz, lambda d: self.z_copy(1, d, r).start())
-        self.f_copy(1, 0, r).start()
-
-    def pass_z(self):
-        for second in range(2):
-            def one(d, second=second):
-                r = self.from_z(second, d)
-                self.z_copy(second, d, r).wait_recv()
-                self.f_copy(second, d, r).start()
-
-            each(1, self.me.nz, one)
-
-    def arrive(self):
-        for second in range(2):
-            each(0, self.me.nz, lambda d, second=second: self.f_copy(
-                second, d, self.from_z(second, d, 1)).wait_recv())
+        self.f_copy(1, r).start()
+
+    def pass_z(self, second):
+        def one(d):
+            r = self.from_z(second, d)
+            self.z_copy(second, d, r).wait_recv()
+            self.f_copy(second, r).start()
+
+        each(1, self.me.nz, one)
+
+    def arrive(self, second):
+        self.f_copy(second, 0, self.me.nz).wait_recv()
 
     def sent(self):
         me = self.me
         self.x_copy(me.row).wait_send()
-        for second in range(2):
-            each(1, me.nz, lambda d, second=second: self.z_copy(second, d, me.row).wait_send())
-            each(0, me.nz, lambda d, second=second: self.f_copy(second, d, me.row).wait_send())
+        at = self.vg.at[pl.ds(0, 2 * (me.nz - 1) * self.block)]
+        remote(at, at, self.z_ss, self.x_rs, (me.row_of(me.z, 1 - me.xl, me.core), me.col)).wait_send()
+        self.f_copy(0, 0, 2 * me.nz).wait_send()
 
 
 class LeftGather:
@@ -140,35 +134,33 @@
         me = self.me
         return remote(self.wg.at[c], self.wg.at[c], self.x_ss, self.x_rs, (me.row, me.col_of(1 - me.xh, me.y)))
 
-    def y_copy(self, second, d, c):
-        me = self.me
-        i = second * (me.ny - 1) + d - 1
+    def y_copy(self, d, c):
+        me = self.me
         to = (me.row, me.col_of(me.xh, me.y_at(d)))
-        return remote(self.wg.at[c], self.wg.at[c], self.y_ss.at[i], self.y_rs.at[i], to)
+        return remote(self.wg.at[c], self.wg.at[c], self.y_ss, self.y_rs, to)
+
+    def y_all(self):
+        me = self.me
+        at = self.wg.at[pl.ds(0, 2 * (me.ny - 1))]
+        return remote(at, at, self.y_ss, self.y_rs, (me.row, me.col_of(1 - me.xh, me.y)))
 
     def start(self):
         me = self.me
         self.x_copy(me.col).start()
-        each(1, me.ny, lambda d: self.y_copy(0, d, me.col).start())
+        each(1, me.ny, lambda d: self.y_copy(d, me.col).start())
 
     def pass_x(self):
         me = self.me
         c = me.col_of(1 - me.xh, me.y)
         self.x_copy(c).wait_recv()
-        each(1, me.ny, lambda d: self.y_copy(1, d, c).start())
+        each(1, me.ny, lambda d: self.y_copy(d, c).start())
 
     def arrive(self):
-        me = self.me
-        for second in range(2):
-            xh = 1 - me.xh if second else me.xh
-            each(1, me.ny, lambda d, second=second, xh=xh: self.y_copy(
-                second, d, me.col_of(xh, me.y_at(-d))).wait_recv())
+        self.y_all().wait_recv()
 
     def sent(self):
-        me = self.me
-        self.x_copy(me.col).wait_send()
-        for second in range(2):
-            each(1, me.ny, lambda d, second=second: self.y_copy(second, d, me.col).wait_send())
+        self.x_copy(self.me.col).wait_send()
+        self.y_all().wait_send()
 
 
 class Exchange:
@@ -184,20 +176,26 @@
     def copy(self, d, slot):
         me = self.me
         to = (self.at(d), me.col) if self.along_row else (me.row, self.at(d))
-        return remote(self.pick(self.at(d)), self.slots.at[slot], self.ss.at[d - 1], self.rs.at[d - 1], to)
+        return remote(self.pick(self.at(d)), self.slots.at[slot], self.ss, self.rs, to)
 
     def start(self):
-        each(1, self.size, lambda d: self.copy(d, self.mine).start())
+        each(1, self.size, lambda d: self.copy(d, self.mine).start(), True)
+
+    def all(self):
+        me = self.me
+        at = self.slots.at[pl.ds(0, self.size - 1)]
+        to = (self.at(1), me.col) if self.along_row else (me.row, self.at(1))
+        return remote(at, at, self.ss, self.rs, to)
 
     def total(self):
-        each(1, self.size, lambda d: self.copy(d, self.at(-d)).wait_recv())
+        self.all().wait_recv()
         total = self.slots[0]
         for i in range(1, self.size):
             total += self.slots[i]
         return total
 
     def sent(self):
-        each(1, self.size, lambda d: self.copy(d, self.mine).wait_send())
+        self.all().wait_send()
 
 
 def gather_kernel(nr, nc, codes, right, left, scale_row, vg, wg, got, got_row, *sems):
@@ -213,29 +211,38 @@
     got_row[me.row] = codes[me.row]
 
     def c1_copy(d, slot):
-        return remote(codes.at[me.row_at(d)], got_row.at[slot], c1_ss.at[d - 1], c1_rs.at[d - 1],
-                      (me.row_at(d), me.col))
+        return remote(codes.at[me.row_at(d)], got_row.at[slot], c1_ss, c1_rs, (me.row_at(d), me.col))
 
     def c2_copy(d, slot):
-        return remote(got_row, got.at[slot], c2_ss.at[d - 1], c2_rs.at[d - 1], (me.row, me.col_at(d)))
+        return remote(got_row, got.at[slot], c2_ss, c2_rs, (me.row, me.col_at(d)))
+
+    def c1_all():
+        at = got_row.at[pl.ds(0, nr - 1)]
+        return remote(at, at, c1_ss, c1_rs, (me.row_at(1), me.col))
+
+    def c2_all():
+        at = got.at[pl.ds(0, nc - 1)]
+        return remote(at, at, c2_ss, c2_rs, (me.row, me.col_at(1)))
 
     hold()
     each(1, nr, lambda d: c1_copy(d, me.row).start())
     v.start()
     w.start()
-    each(1, nr, lambda d: c1_copy(d, me.row_at(-d)).wait_recv())
+    c1_all().wait_recv()
     each(1, nc, lambda d: c2_copy(d, me.col).start())
     got[me.col] = got_row[...]
     v.pass_x()
     w.pass_x()
-    v.pass_z()
-    each(1, nc, lambda d: c2_copy(d, me.col_at(-d)).wait_recv())
+    v.pass_z(0)
+    v.pass_z(1)
+    c2_all().wait_recv()
     w.arrive()
-    v.arrive()
+    v.arrive(0)
+    v.arrive(1)
     v.sent()
     w.sent()
-    each(1, nr, lambda d: c1_copy(d, me.row).wait_send())
-    each(1, nc, lambda d: c2_copy(d, me.col).wait_send())
+    c1_all().wait_send()
+    c2_all().wait_send()
 
 
 def krylov_kernel(
@@ -260,22 +267,39 @@
      n1_ss, n1_rs, n2_ss, n2_rs) = sems[10:]
 
     def r_copy(d):
-        return remote(r_send.at[d - 1], r_recv.at[d - 1], r_ss.at[d - 1], r_rs.at[d - 1], (row, me.col_at(d)))
+        return remote(r_send.at[d - 1], r_recv.at[d - 1], r_ss, r_rs.at[d - 1], (row, me.col_at(d)))
+
+    def r_sent():
+        remote(r_send, r_recv, r_ss, r_rs.at[0], (row, me.col_at(1))).wait_send()
 
     def s_copy(e):
         to = (me.row_of(me.z, me.xl, 1 - me.core), col)
-        return remote(sib_send.at[e], sib_recv.at[e], s_ss.at[e], s_rs.at[e], to)
+        return remote(sib_send.at[e], sib_recv.at[e], s_ss, s_rs.at[e], to)
+
+    def s_sent():
+        remote(sib_send, sib_recv, s_ss, s_rs.at[0], (me.row_of(me.z, me.xl, 1 - me.core), col)).wait_send()
 
     def l_copy(i):
         to = (me.row_of(me.z_at(i % (nz - 1) + 1), me.xl, me.core), col)
-        return remote(l_send.at[i], l_recv.at[i], l_ss.at[i], l_rs.at[i], to)
+        return remote(l_send.at[i], l_recv.at[i], l_ss, l_rs.at[i // (nz - 1)], to)
+
+    def l_sent():
+        remote(l_send, l_recv, l_ss, l_rs.at[0], (me.row_of(me.z, 1 - me.xl, me.core), col)).wait_send()
+
+    def l_arrive(home):
+        at = l_recv.at[pl.ds(home * (nz - 1), nz - 1)]
+        remote(at, at, l_ss, l_rs.at[home], (me.row_of(me.z, 1 - me.xl, me.core), col)).wait_recv()
 
     def x_copy():
         return remote(x_send, x_recv, x_ss, x_rs, (me.row_of(me.z, 1 - me.xl, me.core), col))
 
     def h3_copy(d, slot):
         at = h_full.at[span(slot, h_rows)]
-        return remote(at, at, h3_ss.at[d - 1], h3_rs.at[d - 1], (row, me.col_at(d)))
+        return remote(at, at, h3_ss, h3_rs, (row, me.col_at(d)))
+
+    def h3_all():
+        at = h_full.at[pl.ds(0, (nc - 1) * h_rows)]
+        return remote(at, at, h3_ss, h3_rs, (row, me.col_at(1)))
 
     h1 = Exchange(me, False, h_loc, h_from_col, h1_ss, h1_rs, lambda i: h_loc.at[span(i, h_rows)])
     h2 = Exchange(me, True, h_part, h_from_row, h2_ss, h2_rs)
@@ -307,6 +331,25 @@
     def right_part(c):
         return jnp.dot(ta[span(c, block)], vg[...], preferred_element_type=F32)
 
+    def right_half(c, xl):
+        total = None
+        for z in range(nz):
+            at = span(2 * z + xl, 2 * block)
+            part = jnp.dot(ta[span(c, block), at], vg[at], preferred_element_type=F32)
+            total = part if total is None else total + part
+        return total
+
+    def drain():
+        r_sent()
+        s_sent()
+        l_sent()
+        x_copy().wait_send()
+        h1.sent()
+        h2.sent()
+        h3_all().wait_send()
+        n1.sent()
+        n2.sent()
+
     def left_part(r):
         rows = jnp.concatenate([wg[c] for c in range(nc)], axis=1)
         return jnp.dot(rows, ta[:, span(r, block)], preferred_element_type=F32)
@@ -320,14 +363,29 @@
     for turn in range(ITERS):
         last = turn == ITERS - 1
         if turn:
-            v.arrive()
+            v.pass_x()
+            v.pass_z(0)
+            w.pass_x()
+            drain()
+            v.arrive(0)
+
+            def right_first(d):
+                sib_send[d] = right_half(me.col_at(d), me.xl)
+
+            each(0, nc, right_first)
+            v.pass_z(1)
+            v.arrive(1)
 
         def right_step(d):
-            r_send[d - 1] = right_part(me.col_at(d)).astype(BF16)
+            if turn:
+                r_send[d - 1] = (sib_send[d] + right_half(me.col_at(d), 1 - me.xl)).astype(BF16)
+            else:
+                r_send[d - 1] = right_part(me.col_at(d)).astype(BF16)
             r_copy(d).start()
 
         each(1, nc, right_step)
-        r_new[...] = right_part(col) + diag_col[...] * v_ref[...]
+        own = sib_send[0] + right_half(col, 1 - me.xl) if turn else right_part(col)
+        r_new[...] = own + diag_col[...] * v_ref[...]
 
         if turn:
             w.arrive()
@@ -367,23 +425,20 @@
         h_from_row[row] = part
 
         def left_sum(home):
-            def one(d):
-                i = home * (nz - 1) + d
-                l_copy(i).wait_recv()
-                l_keep[home] += l_recv[i].astype(F32)
-
-            each(0, nz - 1, one)
-
-        left_sum(0)
-        x_send[...] = l_keep[0]
+            l_arrive(home)
+            total = l_keep[home]
+            for d in range(nz - 1):
+                total += l_recv[home * (nz - 1) + d].astype(F32)
+            return total
+
+        x_send[...] = left_sum(0)
         x_copy().start()
 
         h_full[span(col, h_rows)] = h2.total() * (1.0 / order)
-        each(1, nc, lambda d: h3_copy(d, col).start())
+        each(1, nc, lambda d: h3_copy(d, col).start(), True)
         scaled = scale_row[...] * wt[...]
-        left_sum(1)
-        lt_new[...] = l_keep[1] + diag_row[...] * scaled
-        each(1, nc, lambda d: h3_copy(d, me.col_at(-d)).wait_recv())
+        lt_new[...] = left_sum(1) + diag_row[...] * scaled
+        h3_all().wait_recv()
 
         project = h_full[...]
         rest = r_new[...] - jnp.dot(v_ref[...], project, precision=HIGHEST, preferred_element_type=F32)
@@ -402,19 +457,12 @@
         n2.start()
         n_from_col[col] = n_part[...]
 
-        if turn:
+        if last:
             v.sent()
             w.sent()
-        each(1, nc, lambda d: r_copy(d).wait_send())
-        each(0, 2 * nz, lambda e: s_copy(e).wait_send())
-        each(0, 2 * (nz - 1), lambda i: l_copy(i).wait_send())
-        x_copy().wait_send()
-        h1.sent()
-        h2.sent()
-        each(1, nc, lambda d: h3_copy(d, col).wait_send())
-        n1.sent()
         total = n2.total()
-        n2.sent()
+        if last:
+            drain()
         norms = norm_of(total)
         if last:
             norm_out[...] = norms
@@ -428,9 +476,6 @@
             wt[...] = w_new
             wg[col] = (scale_row[...] * w_new).astype(BF16)
             w.start()
-            v.pass_x()
-            w.pass_x()
-            v.pass_z()
 
 
 def finish_kernel(r_ref, lt_ref, norm_ref, h_ref, v_out, w_out, h_out):
@@ -450,12 +495,8 @@
     sem = pltpu.SemaphoreType.DMA
     scale_row = row_scale[None, :]
 
-    def pairs(*counts):
-        return [sem((n,)) if n else sem for n in counts for _ in range(2)]
-
-    gather_sems = pairs(0, 2 * (nz - 1), 2 * nz, 0, 2 * (ny - 1))
-
-    got_tiles = lax.all_to_all(tile_values, ("row", "col"), split_axis=0, concat_axis=0, tiled=True)
+    gather_sems = [sem, sem, sem, sem((2 * (nz - 1),)), sem, sem((2,)), sem, sem, sem, sem]
+
     codes = jnp.pad(slot_codes.reshape(nr, 1, 2 * nc), ((0, 0), (0, 7), (0, 128 - 2 * nc)))
     vg, wg, got = pl.pallas_call(
         functools.partial(gather_kernel, nr, nc),
@@ -466,13 +507,16 @@
         ),
         in_specs=[vmem] * 4,
         out_specs=(vmem,) * 3,
-        scratch_shapes=[pltpu.VMEM((nr, 8, 128), jnp.int32)] + gather_sems + pairs(nr - 1, nc - 1),
+        scratch_shapes=[pltpu.VMEM((nr, 8, 128), jnp.int32)] + gather_sems + [sem] * 4,
         compiler_params=pltpu.CompilerParams(
             collective_id=0, has_side_effects=True, vmem_limit_bytes=16 * 2**20
         ),
         cost_estimate=pl.CostEstimate(flops=10**10, bytes_accessed=10**7, transcendentals=0),
         name="gather",
     )(codes, right_start, left_start, scale_row)
+
+    tile_values, got = lax.optimization_barrier((tile_values, got))
+    got_tiles = lax.all_to_all(tile_values, ("row", "col"), split_axis=0, concat_axis=0, tiled=True)
 
     got = lax.dynamic_slice_in_dim(got[:, :, 0, :], 2 * lax.axis_index("col"), 2, axis=2)
     got_codes = jnp.transpose(got, (1, 0, 2)).reshape(slot_total)
@@ -520,9 +564,8 @@
         ]
         + [sem] * 3
         + gather_sems
-        + pairs(
-            nc - 1, 2 * nz, 2 * (nz - 1), 0, nc - 1, nr - 1, nc - 1, nr - 1, nc - 1
-        ),
+        + [sem, sem((nc - 1,)), sem, sem((2 * nz,)), sem, sem((2,))]
+        + [sem] * 12,
         compiler_params=pltpu.CompilerParams(
             collective_id=1, has_side_effects=True, vmem_limit_bytes=58 * 2**20
         ),

time: 269 us -> 271 us (level)
  waiting for transfers between devices: 0.01 us -> 97.1 us
  Pallas kernels: 251 us -> 157 us
  starting transfers between devices: 12 us -> 7.07 us
  local copies, waits for them, and re-layouts: 4.47 us -> 7.7 us
    all_to_all x1, waiting for transfers between devices: 0.01 us -> 97.1 us  [local(): lax.all_to_all(tile_values, ('row', 'col'), split_axis=0, concat_axis=0,...]
    pallas_call x1, Pallas kernels: 118 us -> 26.5 us  [local(): pl.pallas_call(functools.partial(gather_kernel, nr, nc), out_shape=(jax.S...]
    all_to_all x1, starting transfers between devices: 12 us -> 7.07 us  [local(): lax.all_to_all(tile_values, ('row', 'col'), split_axis=0, concat_axis=0,...]
  transfers between devices with their start and end apart: 1 -> 1, of which waited for: 0 -> 1; matrix products, arithmetic and copies ran while one was open for 1% -> 1% of each run, Pallas kernels for 44% -> 0%
where the time goes in v4:
time: 271 us
  Pallas kernels  157 us (58%)
  waiting for transfers between devices  97.1 us (36%)
  local copies, waits for them, and re-layouts  7.7 us (3%)
  starting transfers between devices  7.07 us (3%)
    pallas_call x1, Pallas kernels, local(): pl.pallas_call(functools.partial(krylov_kernel, nr, nc, order), out_shape...  129 us
    all_to_all x1, waiting for transfers between devices, local(): lax.all_to_all(tile_values, ('row', 'col'), split_axis=0, concat_axis=0,...  97.1 us
    pallas_call x1, Pallas kernels, local(): pl.pallas_call(functools.partial(gather_kernel, nr, nc), out_shape=(jax.S...  26.5 us
    all_to_all x1, starting transfers between devices, local(): lax.all_to_all(tile_values, ('row', 'col'), split_axis=0, concat_axis=0,...  7.07 us
  transfers between devices with their start and end apart: 1, of which 1 were waited for; matrix products, arithmetic and copies ran while one was open for 1% of the time, Pallas kernels for 0%

profile of v4, /device:TPU:1, one launch (start us, length us, event | category | flops | bytes accessed | tf_op | source)
XLA Modules:
  0.0 270.8 jit_solution(15630482325624893301)
XLA Ops:
  0.6 0.8 reshape.11
  1.4 0.0 copy-start.2
  1.4 0.9 copy-done.2
  2.4 0.0 copy-start.3
  2.4 0.9 copy-done.3
  3.3 0.0 copy-start.4
  3.3 0.7 copy-done.4
  4.0 26.5 %gather.1 = (bf16[4096,256]{1,0:T(8,128)(2,1)S(1)}, bf16[8,256,256]{2,1,0:T(8,128)(2,1)S(1)}, s32[8,16,8,128]{3,2,1,0:T(8,128)S(1)}) custom-call(s32[16,8,128]{2,1,0:T(8,128)S(1)} %pad.4.codes, f32[256,256]{1,0:T(8,128)S(1)} %copy-done.2, f32[256,256]{1,0:T(8,128)S(1)} %copy-done.3, f32[1,256]{1,0:T(1,128)S(1)} %bitcast.10), custom_call_target="tpu_custom_call" | custom-call | flops 10000000000 | bytes 10000000 | tf_op jit(solution)/shard_map/gather/pallas_call | solution.py:501
  30.5 0.0 copy-start
  30.5 1.4 copy-done
  31.9 1.0 copy-done.1
  32.9 0.0 copy-start.5
  32.9 7.1 %all-to-all-start = ((bf16[256,128,128]{2,1,0:T(8,128)(2,1)}), bf16[256,128,128]{2,1,0:T(8,128)(2,1)}, u32[]{:S(2)}, u32[]{:S(2)}) async-start(bf16[256,128,128]{2,1,0:T(8,128)(2,1)} %param.6), calls=%async_computation | async-start | bytes 16777216 | tf_op jit(solution)/shard_map/all_to_all | solution.py:519
  39.9 0.0 copy-done.5
  40.0 0.8 copy.18.scale_col
  40.8 0.0 copy-done.6
  40.8 0.8 copy.17.diag_col
  41.6 0.2 constant_dynamic-slice_fusion
  41.8 0.1 eq.15
  42.0 0.2 select_reduce_fusion
  42.1 0.6 compare_select_fusion.slots_ref
  42.7 97.1 %all-to-all-done.tiles_hbm = bf16[256,128,128]{2,1,0:T(8,128)(2,1)} async-done(((bf16[256,128,128]{2,1,0:T(8,128)(2,1)}), bf16[256,128,128]{2,1,0:T(8,128)(2,1)}, u32[]{:S(2)}, u32[]{:S(2)}) %all-to-all-start) | async-done | bytes 8388640 | tf_op jit(solution)/shard_map/all_to_all | solution.py:519
  139.8 128.7 %krylov.1 = (f32[256,256]{1,0:T(8,128)}, f32[256,256]{1,0:T(8,128)}, f32[8,256]{1,0:T(8,128)}, f32[2,256,256]{2,1,0:T(8,128)}) custom-call(s32[512]{0:T(512)} %compare_select_fusion.slots_ref, bf16[256,128,128]{2,1,0:T(8,128)(2,1)} %all-to-all-done.tiles_hbm, bf16[4096,256]{1,0:T(8,128)(2,1)} %copy-done, bf16[8,256,256]{2,1,0:T(8,128)(2,1)} %copy-done.1, ...), custom_call_target="tpu_custom_call" | custom-call | tf_op jit(solution)/shard_map/krylov/pallas_call | solution.py:529
  268.5 2.3 finish.1
  (5 shorter events, 0.1 us)
Async XLA Ops:
  1.4 1.0 copy-start.2
  2.4 0.9 copy-start.3
  3.3 0.7 copy-start.4
  30.5 1.4 copy-start
  31.9 1.0 copy-start.1
  32.9 7.1 %copy-start.5 = (f32[256]{0:T(256)S(1)}, f32[256]{0:T(256)}, u32[]{:S(2)}) copy-start(f32[256]{0:T(256)} %param.11) | copy-start | bytes 3076
  32.9 7.9 %copy-start.6 = (f32[256]{0:T(256)S(1)}, f32[256]{0:T(256)}, u32[]{:S(2)}) copy-start(f32[256]{0:T(256)} %param.10) | copy-start | bytes 3076
  32.9 106.9 %all-to-all-start = ((bf16[256,128,128]{2,1,0:T(8,128)(2,1)}), bf16[256,128,128]{2,1,0:T(8,128)(2,1)}, u32[]{:S(2)}, u32[]{:S(2)}) async-start(bf16[256,128,128]{2,1,0:T(8,128)(2,1)} %param.6), calls=%async_computation | async-start | bytes 16777216 | tf_op jit(solution)/shard_map/all_to_all | solution.py:519

commit v5 on v4

--- a/solution.py
+++ b/solution.py
@@ -19,12 +19,12 @@
     return pl.ds(pl.multiple_of(index * size, size), size)
 
 
-def each(low, high, body, unroll=False):
+def each(low, high, body):
     def step(i, carry):
         body(i)
         return carry
 
-    lax.fori_loop(low, high, step, 0, unroll=unroll)
+    lax.fori_loop(low, high, step, 0)
 
 
 def remote(src, dst, send, recv, to):
@@ -179,7 +179,7 @@
         return remote(self.pick(self.at(d)), self.slots.at[slot], self.ss, self.rs, to)
 
     def start(self):
-        each(1, self.size, lambda d: self.copy(d, self.mine).start(), True)
+        each(1, self.size, lambda d: self.copy(d, self.mine).start())
 
     def all(self):
         me = self.me
@@ -198,16 +198,9 @@
         self.all().wait_send()
 
 
-def gather_kernel(nr, nc, codes, right, left, scale_row, vg, wg, got, got_row, *sems):
+def codes_kernel(nr, nc, codes, got, got_row, c1_ss, c1_rs, c2_ss, c2_rs):
     me = Place(nr, nc)
     hold = me.greet()
-    block = right.shape[0]
-    v = RightGather(me, vg, block, sems[:6])
-    w = LeftGather(me, wg, sems[6:10])
-    c1_ss, c1_rs, c2_ss, c2_rs = sems[10:14]
-    start_right = right[...]
-    vg[span(me.row, block)] = start_right.astype(BF16)
-    wg[me.col] = (scale_row[...] * jnp.transpose(start_right + left[...])).astype(BF16)
     got_row[me.row] = codes[me.row]
 
     def c1_copy(d, slot):
@@ -226,34 +219,23 @@
 
     hold()
     each(1, nr, lambda d: c1_copy(d, me.row).start())
-    v.start()
-    w.start()
     c1_all().wait_recv()
     each(1, nc, lambda d: c2_copy(d, me.col).start())
     got[me.col] = got_row[...]
-    v.pass_x()
-    w.pass_x()
-    v.pass_z(0)
-    v.pass_z(1)
     c2_all().wait_recv()
-    w.arrive()
-    v.arrive(0)
-    v.arrive(1)
-    v.sent()
-    w.sent()
     c1_all().wait_send()
     c2_all().wait_send()
 
 
 def krylov_kernel(
     nr, nc, order,
-    slots_ref, tiles_hbm, vg_hbm, wg_hbm, right_ref, left_ref, diag_col, diag_row, scale_col, scale_row,
+    slots_ref, tiles_hbm, right_ref, left_ref, diag_col, diag_row, scale_col, scale_row,
     r_new, lt_new, norm_out, h_out,
     tiles, ta, vg, wg, v_ref, wt,
     r_send, r_recv, sib_send, sib_recv, l_send, l_recv, l_keep, x_send, x_recv,
     h_loc, h_part, h_from_row, h_from_col, h_full,
     n_loc, n_part, n_from_row, n_from_col,
-    tile_sem, vg_sem, wg_sem, *sems,
+    tile_sem, *sems,
 ):
     me = Place(nr, nc)
     row, col, nz = me.row, me.col, me.nz
@@ -308,28 +290,25 @@
 
     load = pltpu.make_async_copy(tiles_hbm, tiles.at[pl.ds(0, slot_total)], tile_sem)
     load.start()
-    load_vg = pltpu.make_async_copy(vg_hbm, vg, vg_sem)
-    load_vg.start()
-    load_wg = pltpu.make_async_copy(wg_hbm, wg, wg_sem)
-    load_wg.start()
     hold = me.greet()
-    wt[...] = jnp.transpose(right_ref[...] + left_ref[...])
     v_ref[...] = right_ref[...]
+    vg[span(row, block)] = right_ref[...].astype(BF16)
+    w_first = jnp.transpose(right_ref[...] + left_ref[...])
+    wt[...] = w_first
+    wg[col] = (scale_row[...] * w_first).astype(BF16)
+    hold()
+    v.start()
+    w.start()
     n_loc[...] = jnp.zeros_like(n_loc)
     tiles[slot_total] = jnp.zeros((tile, tile), BF16)
     load.wait()
+    v.pass_x()
 
     def one_row(a):
         for b in range(2 * nr):
             ta[span(a, tile), b * tile : (b + 1) * tile] = tiles[slots_ref[a * 2 * nr + b]]
 
     each(0, 2 * nc, one_row)
-    load_vg.wait()
-    load_wg.wait()
-    hold()
-
-    def right_part(c):
-        return jnp.dot(ta[span(c, block)], vg[...], preferred_element_type=F32)
 
     def right_half(c, xl):
         total = None
@@ -364,31 +343,27 @@
         last = turn == ITERS - 1
         if turn:
             v.pass_x()
-            v.pass_z(0)
-            w.pass_x()
+        v.pass_z(0)
+        w.pass_x()
+        if turn:
             drain()
-            v.arrive(0)
-
-            def right_first(d):
-                sib_send[d] = right_half(me.col_at(d), me.xl)
-
-            each(0, nc, right_first)
-            v.pass_z(1)
-            v.arrive(1)
+        v.arrive(0)
+
+        def right_first(d):
+            sib_send[d] = right_half(me.col_at(d), me.xl)
+
+        each(0, nc, right_first)
+        v.pass_z(1)
+        v.arrive(1)
 
         def right_step(d):
-            if turn:
-                r_send[d - 1] = (sib_send[d] + right_half(me.col_at(d), 1 - me.xl)).astype(BF16)
-            else:
-                r_send[d - 1] = right_part(me.col_at(d)).astype(BF16)
+            r_send[d - 1] = (sib_send[d] + right_half(me.col_at(d), 1 - me.xl)).astype(BF16)
             r_copy(d).start()
 
         each(1, nc, right_step)
-        own = sib_send[0] + right_half(col, 1 - me.xl) if turn else right_part(col)
-        r_new[...] = own + diag_col[...] * v_ref[...]
-
-        if turn:
-            w.arrive()
+        r_new[...] = sib_send[0] + right_half(col, 1 - me.xl) + diag_col[...] * v_ref[...]
+
+        w.arrive()
 
         def left_other(e):
             sib_send[e] = left_part(me.row_of(me.z_at(e % nz + 1), xl_of(e // nz), 1 - me.core))
@@ -419,10 +394,6 @@
         h_loc[...] = jnp.dot(wt[...], r_new[...], precision=HIGHEST, preferred_element_type=F32)
         h1.start()
         h_from_col[col] = h_loc[span(col, h_rows)]
-        part = h1.total()
-        h_part[...] = part
-        h2.start()
-        h_from_row[row] = part
 
         def left_sum(home):
             l_arrive(home)
@@ -433,9 +404,15 @@
 
         x_send[...] = left_sum(0)
         x_copy().start()
+        part = h1.total()
+        h_part[...] = part
+        h2.start()
+        h_from_row[row] = part
+        v.sent()
+        w.sent()
 
         h_full[span(col, h_rows)] = h2.total() * (1.0 / order)
-        each(1, nc, lambda d: h3_copy(d, col).start(), True)
+        each(1, nc, lambda d: h3_copy(d, col).start())
         scaled = scale_row[...] * wt[...]
         lt_new[...] = left_sum(1) + diag_row[...] * scaled
         h3_all().wait_recv()
@@ -457,9 +434,6 @@
         n2.start()
         n_from_col[col] = n_part[...]
 
-        if last:
-            v.sent()
-            w.sent()
         total = n2.total()
         if last:
             drain()
@@ -497,26 +471,20 @@
 
     gather_sems = [sem, sem, sem, sem((2 * (nz - 1),)), sem, sem((2,)), sem, sem, sem, sem]
 
+    got_tiles = lax.all_to_all(tile_values, ("row", "col"), split_axis=0, concat_axis=0, tiled=True)
     codes = jnp.pad(slot_codes.reshape(nr, 1, 2 * nc), ((0, 0), (0, 7), (0, 128 - 2 * nc)))
-    vg, wg, got = pl.pallas_call(
-        functools.partial(gather_kernel, nr, nc),
-        out_shape=(
-            jax.ShapeDtypeStruct((nr * rows, ports), BF16),
-            jax.ShapeDtypeStruct((nc, ports, rows), BF16),
-            jax.ShapeDtypeStruct((nc, nr, 8, 128), jnp.int32),
-        ),
-        in_specs=[vmem] * 4,
-        out_specs=(vmem,) * 3,
-        scratch_shapes=[pltpu.VMEM((nr, 8, 128), jnp.int32)] + gather_sems + [sem] * 4,
+    got = pl.pallas_call(
+        functools.partial(codes_kernel, nr, nc),
+        out_shape=jax.ShapeDtypeStruct((nc, nr, 8, 128), jnp.int32),
+        in_specs=[vmem],
+        out_specs=vmem,
+        scratch_shapes=[pltpu.VMEM((nr, 8, 128), jnp.int32)] + [sem] * 4,
         compiler_params=pltpu.CompilerParams(
             collective_id=0, has_side_effects=True, vmem_limit_bytes=16 * 2**20
         ),
         cost_estimate=pl.CostEstimate(flops=10**10, bytes_accessed=10**7, transcendentals=0),
-        name="gather",
-    )(codes, right_start, left_start, scale_row)
-
-    tile_values, got = lax.optimization_barrier((tile_values, got))
-    got_tiles = lax.all_to_all(tile_values, ("row", "col"), split_axis=0, concat_axis=0, tiled=True)
+        name="codes",
+    )(codes)
 
     got = lax.dynamic_slice_in_dim(got[:, :, 0, :], 2 * lax.axis_index("col"), 2, axis=2)
     got_codes = jnp.transpose(got, (1, 0, 2)).reshape(slot_total)
@@ -534,7 +502,7 @@
             jax.ShapeDtypeStruct((8, ports), F32),
             jax.ShapeDtypeStruct((ITERS, ports, ports), F32),
         ),
-        in_specs=[pl.BlockSpec(memory_space=pltpu.SMEM)] + [any_space] * 3 + [vmem] * 6,
+        in_specs=[pl.BlockSpec(memory_space=pltpu.SMEM)] + [any_space] + [vmem] * 6,
         out_specs=(vmem,) * 4,
         scratch_shapes=[
             pltpu.VMEM((slot_total + 1, tile, tile), BF16),
@@ -562,7 +530,7 @@
             pltpu.VMEM((nr, 8, ports), F32),
             pltpu.VMEM((nc, 8, ports), F32),
         ]
-        + [sem] * 3
+        + [sem]
         + gather_sems
         + [sem, sem((nc - 1,)), sem, sem((2 * nz,)), sem, sem((2,))]
         + [sem] * 12,
@@ -571,7 +539,7 @@
         ),
         name="krylov",
     )(
-        slots, got_tiles, vg, wg, right_start, left_start,
+        slots, got_tiles, right_start, left_start,
         node_diagonal[:, None], node_diagonal[None, :], row_scale[:, None], scale_row,
     )
     return tuple(

time: 271 us -> 263 us (0.970)
  waiting for transfers between devices: 97.1 us -> 0.01 us
  Pallas kernels: 157 us -> 248 us
  local copies, waits for them, and re-layouts: 7.7 us -> 2.12 us
  starting transfers between devices: 7.07 us -> 12 us
    all_to_all x1, waiting for transfers between devices: 97.1 us -> 0.01 us  [local(): lax.all_to_all(tile_values, ('row', 'col'), split_axis=0, concat_axis=0,...]
    pallas_call x1, Pallas kernels: 26.5 us -> 107 us  [local(): pl.pallas_call(functools.partial(codes_kernel, nr, nc), out_shape=jax.Sha...]
    pallas_call x1, Pallas kernels: 129 us -> 138 us  [local(): pl.pallas_call(functools.partial(krylov_kernel, nr, nc, order), out_shape...]
    unnamed x14 -> x6, local copies, waits for them, and re-layouts: 4.92 us -> 0.02 us
    all_to_all x1, starting transfers between devices: 7.07 us -> 12 us  [local(): lax.all_to_all(tile_values, ('row', 'col'), split_axis=0, concat_axis=0,...]
  transfers between devices with their start and end apart: 1 -> 1, of which waited for: 1 -> 0; matrix products, arithmetic and copies ran while one was open for 1% -> 1% of each run, Pallas kernels for 0% -> 41%
where the time goes in v5:
time: 263 us
  Pallas kernels  248 us (94%)
  starting transfers between devices  12 us (5%)
    pallas_call x1, Pallas kernels, local(): pl.pallas_call(functools.partial(krylov_kernel, nr, nc, order), out_shape...  138 us
    pallas_call x1, Pallas kernels, local(): pl.pallas_call(functools.partial(codes_kernel, nr, nc), out_shape=jax.Sha...  107 us
    all_to_all x1, starting transfers between devices, local(): lax.all_to_all(tile_values, ('row', 'col'), split_axis=0, concat_axis=0,...  12 us
  transfers between devices with their start and end apart: 1, of which 0 were waited for; matrix products, arithmetic and copies ran while one was open for 1% of the time, Pallas kernels for 41%

profile of v5, /device:TPU:1, one launch (start us, length us, event | category | flops | bytes accessed | tf_op | source)
XLA Modules:
  0.0 263.1 jit_solution(5580018960577954256)
XLA Ops:
  0.6 0.0 copy-start.2
  0.6 0.0 copy-start.1
  0.7 0.0 copy-start
  0.7 12.0 %all-to-all-start = ((bf16[256,128,128]{2,1,0:T(8,128)(2,1)}), bf16[256,128,128]{2,1,0:T(8,128)(2,1)}, u32[]{:S(2)}, u32[]{:S(2)}) async-start(bf16[256,128,128]{2,1,0:T(8,128)(2,1)} %param.6), calls=%async_computation | async-start | bytes 16777216 | tf_op jit(solution)/shard_map/all_to_all | solution.py:474
  12.6 0.0 copy-done.2
  12.6 0.1 reshape.11
  12.8 0.0 copy-done.1
  12.8 0.8 copy.18.scale_col
  13.6 0.0 copy-done
  13.6 0.8 copy.17.diag_col
  14.4 107.1 %codes.1 = s32[8,16,8,128]{3,2,1,0:T(8,128)S(1)} custom-call(s32[16,8,128]{2,1,0:T(8,128)S(1)} %pad.4.codes), custom_call_target="tpu_custom_call" | custom-call | flops 10000000000 | bytes 10000000 | tf_op jit(solution)/shard_map/codes/pallas_call | solution.py:476
  121.5 0.2 constant_dynamic-slice_fusion
  121.7 0.1 eq.15
  121.9 0.2 select_reduce_fusion
  122.0 0.6 compare_select_fusion.slots_ref
  122.6 0.0 all-to-all-done.tiles_hbm
  122.6 138.2 %krylov.1 = (f32[256,256]{1,0:T(8,128)}, f32[256,256]{1,0:T(8,128)}, f32[8,256]{1,0:T(8,128)}, f32[2,256,256]{2,1,0:T(8,128)}) custom-call(s32[512]{0:T(512)} %compare_select_fusion.slots_ref, bf16[256,128,128]{2,1,0:T(8,128)(2,1)} %all-to-all-done.tiles_hbm, f32[256,256]{1,0:T(8,128)} %right_ref.1, f32[256,256]{1,0:T(8,128)} %left_ref.1, ...), custom_call_target="tpu_custom_call" | custom-call | tf_op jit(solution)/shard_map/krylov/pallas_call | solution.py:497
  260.8 2.3 finish.1
  (3 shorter events, 0.1 us)
Async XLA Ops:
  0.6 12.0 %copy-start.2 = (s32[256]{0:T(256)S(1)}, s32[256]{0:T(256)}, u32[]{:S(2)}) copy-start(s32[256]{0:T(256)} %param.7) | copy-start | bytes 3076
  0.6 12.1 %copy-start.1 = (f32[256]{0:T(256)S(1)}, f32[256]{0:T(256)}, u32[]{:S(2)}) copy-start(f32[256]{0:T(256)} %param.11) | copy-start | bytes 3076
  0.7 12.9 %copy-start = (f32[256]{0:T(256)S(1)}, f32[256]{0:T(256)}, u32[]{:S(2)}) copy-start(f32[256]{0:T(256)} %param.10) | copy-start | bytes 3076
  0.7 122.0 %all-to-all-start = ((bf16[256,128,128]{2,1,0:T(8,128)(2,1)}), bf16[256,128,128]{2,1,0:T(8,128)(2,1)}, u32[]{:S(2)}, u32[]{:S(2)}) async-start(bf16[256,128,128]{2,1,0:T(8,128)(2,1)} %param.6), calls=%async_computation | async-start | bytes 16777216 | tf_op jit(solution)/shard_map/all_to_all | solution.py:474

commit v6 on v5

--- a/solution.py
+++ b/solution.py
@@ -471,7 +471,6 @@
 
     gather_sems = [sem, sem, sem, sem((2 * (nz - 1),)), sem, sem((2,)), sem, sem, sem, sem]
 
-    got_tiles = lax.all_to_all(tile_values, ("row", "col"), split_axis=0, concat_axis=0, tiled=True)
     codes = jnp.pad(slot_codes.reshape(nr, 1, 2 * nc), ((0, 0), (0, 7), (0, 128 - 2 * nc)))
     got = pl.pallas_call(
         functools.partial(codes_kernel, nr, nc),
@@ -485,6 +484,9 @@
         cost_estimate=pl.CostEstimate(flops=10**10, bytes_accessed=10**7, transcendentals=0),
         name="codes",
     )(codes)
+
+    tile_values, got = lax.optimization_barrier((tile_values, got))
+    got_tiles = lax.all_to_all(tile_values, ("row", "col"), split_axis=0, concat_axis=0, tiled=True)
 
     got = lax.dynamic_slice_in_dim(got[:, :, 0, :], 2 * lax.axis_index("col"), 2, axis=2)
     got_codes = jnp.transpose(got, (1, 0, 2)).reshape(slot_total)

time: 263 us -> 276 us (1.049)
  waiting for transfers between devices: 0.01 us -> 97.1 us
  Pallas kernels: 248 us -> 165 us
    all_to_all x1, waiting for transfers between devices: 0.01 us -> 97.1 us  [local(): lax.all_to_all(tile_values, ('row', 'col'), split_axis=0, concat_axis=0,...]
    pallas_call x1, Pallas kernels: 107 us -> 19.8 us  [local(): pl.pallas_call(functools.partial(codes_kernel, nr, nc), out_shape=jax.Sha...]
    pallas_call x1, Pallas kernels: 138 us -> 142 us  [local(): pl.pallas_call(functools.partial(krylov_kernel, nr, nc, order), out_shape...]
  transfers between devices with their start and end apart: 1 -> 1, of which waited for: 0 -> 1; matrix products, arithmetic and copies ran while one was open for 1% -> 1% of each run, Pallas kernels for 41% -> 0%
where the time goes in v6:
time: 276 us; the launch traced here: 275 us
  Pallas kernels  165 us (60%)
  waiting for transfers between devices  97.1 us (35%)
  starting transfers between devices  9.62 us (3%)
  local copies, waits for them, and re-layouts  2.79 us (1%)
    pallas_call x1, Pallas kernels, local(): pl.pallas_call(functools.partial(krylov_kernel, nr, nc, order), out_shape...  142 us
    all_to_all x1, waiting for transfers between devices, local(): lax.all_to_all(tile_values, ('row', 'col'), split_axis=0, concat_axis=0,...  97.1 us
    pallas_call x1, Pallas kernels, local(): pl.pallas_call(functools.partial(codes_kernel, nr, nc), out_shape=jax.Sha...  19.8 us
    all_to_all x1, starting transfers between devices, local(): lax.all_to_all(tile_values, ('row', 'col'), split_axis=0, concat_axis=0,...  9.62 us
  transfers between devices with their start and end apart: 1, of which 1 were waited for; matrix products, arithmetic and copies ran while one was open for 1% of the time, Pallas kernels for 0%

profile of v6, /device:TPU:1, one launch (start us, length us, event | category | flops | bytes accessed | tf_op | source)
XLA Modules:
  0.0 275.5 jit_solution(2627076198701099247)
XLA Ops:
  0.6 0.8 reshape.11
  1.4 19.8 %codes.1 = s32[8,16,8,128]{3,2,1,0:T(8,128)S(1)} custom-call(s32[16,8,128]{2,1,0:T(8,128)S(1)} %pad.4.codes), custom_call_target="tpu_custom_call" | custom-call | flops 10000000000 | bytes 10000000 | tf_op jit(solution)/shard_map/codes/pallas_call | solution.py:475
  21.2 0.0 copy-start.1
  21.2 0.0 copy-start
  21.3 9.6 %all-to-all-start = ((bf16[256,128,128]{2,1,0:T(8,128)(2,1)}), bf16[256,128,128]{2,1,0:T(8,128)(2,1)}, u32[]{:S(2)}, u32[]{:S(2)}) async-start(bf16[256,128,128]{2,1,0:T(8,128)(2,1)} %param.6), calls=%async_computation | async-start | bytes 16777216 | tf_op jit(solution)/shard_map/all_to_all | solution.py:489
  30.9 0.0 copy-done.1
  30.9 0.8 copy.18.scale_col
  31.7 0.0 copy-done
  31.7 0.8 copy.17.diag_col
  32.5 0.2 constant_dynamic-slice_fusion
  32.8 0.1 eq.15
  32.9 0.2 select_reduce_fusion
  33.1 0.6 compare_select_fusion.slots_ref
  33.7 97.1 %all-to-all-done.tiles_hbm = bf16[256,128,128]{2,1,0:T(8,128)(2,1)} async-done(((bf16[256,128,128]{2,1,0:T(8,128)(2,1)}), bf16[256,128,128]{2,1,0:T(8,128)(2,1)}, u32[]{:S(2)}, u32[]{:S(2)}) %all-to-all-start) | async-done | bytes 8388640 | tf_op jit(solution)/shard_map/all_to_all | solution.py:489
  130.7 142.4 %krylov.1 = (f32[256,256]{1,0:T(8,128)}, f32[256,256]{1,0:T(8,128)}, f32[8,256]{1,0:T(8,128)}, f32[2,256,256]{2,1,0:T(8,128)}) custom-call(s32[512]{0:T(512)} %compare_select_fusion.slots_ref, bf16[256,128,128]{2,1,0:T(8,128)(2,1)} %all-to-all-done.tiles_hbm, f32[256,256]{1,0:T(8,128)} %right_ref.1, f32[256,256]{1,0:T(8,128)} %left_ref.1, ...), custom_call_target="tpu_custom_call" | custom-call | tf_op jit(solution)/shard_map/krylov/pallas_call | solution.py:499
  273.2 2.3 finish.1
  (3 shorter events, 0.1 us)
Async XLA Ops:
  21.2 9.7 %copy-start.1 = (f32[256]{0:T(256)S(1)}, f32[256]{0:T(256)}, u32[]{:S(2)}) copy-start(f32[256]{0:T(256)} %param.11) | copy-start | bytes 3076
  21.2 10.5 %copy-start = (f32[256]{0:T(256)S(1)}, f32[256]{0:T(256)}, u32[]{:S(2)}) copy-start(f32[256]{0:T(256)} %param.10) | copy-start | bytes 3076
  21.3 109.5 %all-to-all-start = ((bf16[256,128,128]{2,1,0:T(8,128)(2,1)}), bf16[256,128,128]{2,1,0:T(8,128)(2,1)}, u32[]{:S(2)}, u32[]{:S(2)}) async-start(bf16[256,128,128]{2,1,0:T(8,128)(2,1)} %param.6), calls=%async_computation | async-start | bytes 16777216 | tf_op jit(solution)/shard_map/all_to_all | solution.py:489

commit v7 on v5

--- a/solution.py
+++ b/solution.py
@@ -472,13 +472,13 @@
     gather_sems = [sem, sem, sem, sem((2 * (nz - 1),)), sem, sem((2,)), sem, sem, sem, sem]
 
     got_tiles = lax.all_to_all(tile_values, ("row", "col"), split_axis=0, concat_axis=0, tiled=True)
-    codes = jnp.pad(slot_codes.reshape(nr, 1, 2 * nc), ((0, 0), (0, 7), (0, 128 - 2 * nc)))
+    codes = jnp.pad(slot_codes.reshape(nr, 1, 2 * nc), ((0, 0), (0, 0), (0, 128 - 2 * nc)))
     got = pl.pallas_call(
         functools.partial(codes_kernel, nr, nc),
-        out_shape=jax.ShapeDtypeStruct((nc, nr, 8, 128), jnp.int32),
+        out_shape=jax.ShapeDtypeStruct((nc, nr, 1, 128), jnp.int32),
         in_specs=[vmem],
         out_specs=vmem,
-        scratch_shapes=[pltpu.VMEM((nr, 8, 128), jnp.int32)] + [sem] * 4,
+        scratch_shapes=[pltpu.VMEM((nr, 1, 128), jnp.int32)] + [sem] * 4,
         compiler_params=pltpu.CompilerParams(
             collective_id=0, has_side_effects=True, vmem_limit_bytes=16 * 2**20
         ),

time: 263 us -> 262 us (level)
  no operation moved by 1% of the time
where the time goes in v7:
time: 262 us
  Pallas kernels  246 us (94%)
  starting transfers between devices  12 us (5%)
    pallas_call x1, Pallas kernels, local(): pl.pallas_call(functools.partial(krylov_kernel, nr, nc, order), out_shape...  137 us
    pallas_call x1, Pallas kernels, local(): pl.pallas_call(functools.partial(codes_kernel, nr, nc), out_shape=jax.Sha...  107 us
    all_to_all x1, starting transfers between devices, local(): lax.all_to_all(tile_values, ('row', 'col'), split_axis=0, concat_axis=0,...  12 us
  transfers between devices with their start and end apart: 1, of which 0 were waited for; matrix products, arithmetic and copies ran while one was open for 1% of the time, Pallas kernels for 41%

profile of v7, /device:TPU:1, one launch (start us, length us, event | category | flops | bytes accessed | tf_op | source)
XLA Modules:
  0.0 261.8 jit_solution(3985355777811652191)
XLA Ops:
  0.6 0.0 copy-start.2
  0.6 12.0 %all-to-all-start = ((bf16[256,128,128]{2,1,0:T(8,128)(2,1)}), bf16[256,128,128]{2,1,0:T(8,128)(2,1)}, u32[]{:S(2)}, u32[]{:S(2)}) async-start(bf16[256,128,128]{2,1,0:T(8,128)(2,1)} %param.6), calls=%async_computation | async-start | bytes 16777216 | tf_op jit(solution)/shard_map/all_to_all | solution.py:474
  12.6 0.0 copy-done.2
  12.6 0.1 reshape.11
  12.7 0.0 copy-start.1
  12.7 0.0 copy-start
  12.8 106.6 %codes.1 = s32[8,16,1,128]{3,2,1,0:T(1,128)S(1)} custom-call(s32[16,1,128]{2,1,0:T(1,128)S(1)} %pad.4.codes), custom_call_target="tpu_custom_call" | custom-call | flops 10000000000 | bytes 10000000 | tf_op jit(solution)/shard_map/codes/pallas_call | solution.py:476
  119.3 0.2 constant_dynamic-slice_fusion
  119.6 0.1 eq.15
  119.7 0.0 copy-done.1
  119.7 0.8 copy.18.scale_col
  120.5 0.0 copy-done
  120.5 0.8 copy.17.diag_col
  121.3 0.1 select_reduce_fusion
  121.5 0.6 compare_select_fusion.slots_ref
  122.1 0.0 all-to-all-done.tiles_hbm
  122.1 137.4 %krylov.1 = (f32[256,256]{1,0:T(8,128)}, f32[256,256]{1,0:T(8,128)}, f32[8,256]{1,0:T(8,128)}, f32[2,256,256]{2,1,0:T(8,128)}) custom-call(s32[512]{0:T(512)} %compare_select_fusion.slots_ref, bf16[256,128,128]{2,1,0:T(8,128)(2,1)} %all-to-all-done.tiles_hbm, f32[256,256]{1,0:T(8,128)} %right_ref.1, f32[256,256]{1,0:T(8,128)} %left_ref.1, ...), custom_call_target="tpu_custom_call" | custom-call | tf_op jit(solution)/shard_map/krylov/pallas_call | solution.py:497
  259.5 2.3 finish.1
  (2 shorter events, 0.0 us)
Async XLA Ops:
  0.6 12.0 %copy-start.2 = (s32[256]{0:T(256)S(1)}, s32[256]{0:T(256)}, u32[]{:S(2)}) copy-start(s32[256]{0:T(256)} %param.7) | copy-start | bytes 3076
  0.6 121.4 %all-to-all-start = ((bf16[256,128,128]{2,1,0:T(8,128)(2,1)}), bf16[256,128,128]{2,1,0:T(8,128)(2,1)}, u32[]{:S(2)}, u32[]{:S(2)}) async-start(bf16[256,128,128]{2,1,0:T(8,128)(2,1)} %param.6), calls=%async_computation | async-start | bytes 16777216 | tf_op jit(solution)/shard_map/all_to_all | solution.py:474
  12.7 107.0 %copy-start.1 = (f32[256]{0:T(256)S(1)}, f32[256]{0:T(256)}, u32[]{:S(2)}) copy-start(f32[256]{0:T(256)} %param.11) | copy-start | bytes 3076
  12.7 107.8 %copy-start = (f32[256]{0:T(256)S(1)}, f32[256]{0:T(256)}, u32[]{:S(2)}) copy-start(f32[256]{0:T(256)} %param.10) | copy-start | bytes 3076

commit v8 on v7

--- a/solution.py
+++ b/solution.py
@@ -248,8 +248,13 @@
     (r_ss, r_rs, s_ss, s_rs, l_ss, l_rs, x_ss, x_rs, h1_ss, h1_rs, h2_ss, h2_rs, h3_ss, h3_rs,
      n1_ss, n1_rs, n2_ss, n2_rs) = sems[10:]
 
+    def right_to(d):
+        across = (2 * me.ny - d) // me.ny
+        xh = me.xh + across - 2 * me.xh * across
+        return me.col_of(xh, me.y_at(d - me.ny + across * (me.ny - 1)))
+
     def r_copy(d):
-        return remote(r_send.at[d - 1], r_recv.at[d - 1], r_ss, r_rs.at[d - 1], (row, me.col_at(d)))
+        return remote(r_send.at[d - 1], r_recv.at[d - 1], r_ss, r_rs.at[d - 1], (row, right_to(d)))
 
     def r_sent():
         remote(r_send, r_recv, r_ss, r_rs.at[0], (row, me.col_at(1))).wait_send()
@@ -350,14 +355,15 @@
         v.arrive(0)
 
         def right_first(d):
-            sib_send[d] = right_half(me.col_at(d), me.xl)
-
-        each(0, nc, right_first)
+            sib_send[d] = right_half(right_to(d), me.xl)
+
+        each(1, nc, right_first)
+        sib_send[0] = right_half(col, me.xl)
         v.pass_z(1)
         v.arrive(1)
 
         def right_step(d):
-            r_send[d - 1] = (sib_send[d] + right_half(me.col_at(d), 1 - me.xl)).astype(BF16)
+            r_send[d - 1] = (sib_send[d] + right_half(right_to(d), 1 - me.xl)).astype(BF16)
             r_copy(d).start()
 
         each(1, nc, right_step)

time: 262 us -> 260 us (level)
  no operation moved by 1% of the time
where the time goes in v8:
time: 260 us
  Pallas kernels  245 us (94%)
  starting transfers between devices  12 us (5%)
    pallas_call x1, Pallas kernels, local(): pl.pallas_call(functools.partial(krylov_kernel, nr, nc, order), out_shape...  136 us
    pallas_call x1, Pallas kernels, local(): pl.pallas_call(functools.partial(codes_kernel, nr, nc), out_shape=jax.Sha...  107 us
    all_to_all x1, starting transfers between devices, local(): lax.all_to_all(tile_values, ('row', 'col'), split_axis=0, concat_axis=0,...  12 us
  transfers between devices with their start and end apart: 1, of which 0 were waited for; matrix products, arithmetic and copies ran while one was open for 1% of the time, Pallas kernels for 41%

profile of v8, /device:TPU:1, one launch (start us, length us, event | category | flops | bytes accessed | tf_op | source)
XLA Modules:
  0.0 260.1 jit_solution(5008499220984890686)
XLA Ops:
  0.6 0.0 copy-start.2
  0.6 12.0 %all-to-all-start = ((bf16[256,128,128]{2,1,0:T(8,128)(2,1)}), bf16[256,128,128]{2,1,0:T(8,128)(2,1)}, u32[]{:S(2)}, u32[]{:S(2)}) async-start(bf16[256,128,128]{2,1,0:T(8,128)(2,1)} %param.6), calls=%async_computation | async-start | bytes 16777216 | tf_op jit(solution)/shard_map/all_to_all | solution.py:480
  12.6 0.0 copy-done.2
  12.6 0.1 reshape.11
  12.7 0.0 copy-start.1
  12.7 0.0 copy-start
  12.8 106.6 %codes.1 = s32[8,16,1,128]{3,2,1,0:T(1,128)S(1)} custom-call(s32[16,1,128]{2,1,0:T(1,128)S(1)} %pad.4.codes), custom_call_target="tpu_custom_call" | custom-call | flops 10000000000 | bytes 10000000 | tf_op jit(solution)/shard_map/codes/pallas_call | solution.py:482
  119.3 0.2 constant_dynamic-slice_fusion
  119.6 0.1 eq.15
  119.7 0.0 copy-done.1
  119.7 0.8 copy.18.scale_col
  120.5 0.0 copy-done
  120.5 0.8 copy.17.diag_col
  121.3 0.1 select_reduce_fusion
  121.5 0.6 compare_select_fusion.slots_ref
  122.1 0.0 all-to-all-done.tiles_hbm
  122.1 135.8 %krylov.1 = (f32[256,256]{1,0:T(8,128)}, f32[256,256]{1,0:T(8,128)}, f32[8,256]{1,0:T(8,128)}, f32[2,256,256]{2,1,0:T(8,128)}) custom-call(s32[512]{0:T(512)} %compare_select_fusion.slots_ref, bf16[256,128,128]{2,1,0:T(8,128)(2,1)} %all-to-all-done.tiles_hbm, f32[256,256]{1,0:T(8,128)} %right_ref.1, f32[256,256]{1,0:T(8,128)} %left_ref.1, ...), custom_call_target="tpu_custom_call" | custom-call | tf_op jit(solution)/shard_map/krylov/pallas_call | solution.py:503
  257.9 2.3 finish.1
  (2 shorter events, 0.0 us)
Async XLA Ops:
  0.6 12.0 %copy-start.2 = (s32[256]{0:T(256)S(1)}, s32[256]{0:T(256)}, u32[]{:S(2)}) copy-start(s32[256]{0:T(256)} %param.7) | copy-start | bytes 3076
  0.6 121.4 %all-to-all-start = ((bf16[256,128,128]{2,1,0:T(8,128)(2,1)}), bf16[256,128,128]{2,1,0:T(8,128)(2,1)}, u32[]{:S(2)}, u32[]{:S(2)}) async-start(bf16[256,128,128]{2,1,0:T(8,128)(2,1)} %param.6), calls=%async_computation | async-start | bytes 16777216 | tf_op jit(solution)/shard_map/all_to_all | solution.py:480
  12.7 107.0 %copy-start.1 = (f32[256]{0:T(256)S(1)}, f32[256]{0:T(256)}, u32[]{:S(2)}) copy-start(f32[256]{0:T(256)} %param.11) | copy-start | bytes 3076
  12.7 107.8 %copy-start = (f32[256]{0:T(256)S(1)}, f32[256]{0:T(256)}, u32[]{:S(2)}) copy-start(f32[256]{0:T(256)} %param.10) | copy-start | bytes 3076
